TPU v7x, 128 devices: a whole 4x4x4 slice. The times are simulated.
128 devices in a mesh: grp: 4 (over x), dp: 32 (over y, z, core).
Axes of the slice: x: 4, y: 4, z: 4, core: 2. Of those that a mesh axis runs over, the one named last changes fastest.
Arguments:
- blocks: bfloat16 [512, 128, 1280], P(('grp', 'dp')), may hold values from -6 to 6
- cotangent: bfloat16 [512, 128, 1280], P(('grp', 'dp')), may hold values from -6 to 6
- modality: int32 [512], P(('grp', 'dp')), may hold values from 0 to 1, as said below
- time_rank: int32 [512], P(('grp', 'dp')), may hold values from 0 to 3, as said below
- qkv_weight: bfloat16 [2, 1280, 1920], P(None, 'dp'), may hold values from -5 to 5
- out_weight: bfloat16 [2, 640, 1280], P(None, 'dp'), may hold values from -0.25 to 0.25
- norm_gain: bfloat16 [2, 1280], P(None, 'dp'), may hold values from 0.5 to 1.5
Outputs:
- encoded: bfloat16 [512, 128, 1280], P(('grp', 'dp'))
- block_grad: bfloat16 [512, 128, 1280], P(('grp', 'dp'))
- qkv_grad: float32 [4, 1280, 1920], P('grp', 'dp')
- out_grad: float32 [4, 640, 1280], P('grp', 'dp')
- gain_grad: float32 [4, 1280], P('grp', 'dp')
Inputs may be any that keep to these rules, and one draw needn't show every extreme that they name: On one index of dp, chosen by the draw, all blocks of all four grp rows have the same modality. `time_rank`: within each device's 4 blocks, a permutation of 0 to 3.
All inputs are finite; a program needn't handle non-finite values.
Results may differ from a plain program's by a relative error of at most 0.029.
The roundings to bfloat16 on the way count: a program that leaves them out, or rounds other values in their place, can miss the bound.
Values may be sent and summed in bfloat16 or wider, within the bound.
A program may use at most 128 MiB of HBM per device.

v0:
```python
import math

import jax
import jax.numpy as jnp
from jax import lax
from jax.sharding import PartitionSpec as P

A_HEADS = 10
A_SIZE = 64
V_HEADS = 8
V_SIZE = 80
WIN = 128
VWIN = 64
CAP = 2


EPSILON = 1e-05


def from_partner(block, axis, distance):
    count = lax.axis_size(axis)
    route = []
    for low in range(count):
        high = low | 1 << distance
        if high != low and high < count:
            route += [(low, high), (high, low)]
    return lax.ppermute(block, axis, route)


def attend(qkv_rows, out_cot, heads, head_size, window):
    total_rows = qkv_rows.shape[0]
    inner = heads * head_size
    windows = total_rows // window
    shape = (windows, window, heads, head_size)
    query = qkv_rows[:, :inner].reshape(shape)
    keys = qkv_rows[:, inner : 2 * inner].reshape(shape)
    values = qkv_rows[:, 2 * inner :].reshape(shape)
    scale = 1.0 / math.sqrt(head_size)
    scores = jnp.einsum("wqhd,wkhd->whqk", query, keys, preferred_element_type=jnp.float32) * scale
    row_max = jnp.max(scores, axis=-1, keepdims=True)
    exponent = jnp.exp(scores - row_max)
    probs = exponent / jnp.sum(exponent, axis=-1, keepdims=True)
    probs_low = probs.astype(jnp.bfloat16)
    mixed = (
        jnp.einsum("whqk,wkhd->wqhd", probs_low, values, preferred_element_type=jnp.float32)
        .astype(jnp.bfloat16)
        .reshape(total_rows, inner)
    )
    cot_heads = out_cot.reshape(shape)
    d_probs = jnp.einsum("wqhd,wkhd->whqk", cot_heads, values, preferred_element_type=jnp.float32)
    d_values = jnp.einsum(
        "whqk,wqhd->wkhd", probs_low, cot_heads, preferred_element_type=jnp.float32
    ).astype(jnp.bfloat16)
    d_scores = (
        probs * (d_probs - jnp.sum(d_probs * probs, axis=-1, keepdims=True)) * scale
    ).astype(jnp.bfloat16)
    d_query = jnp.einsum(
        "whqk,wkhd->wqhd", d_scores, keys, preferred_element_type=jnp.float32
    ).astype(jnp.bfloat16)
    d_keys = jnp.einsum(
        "whqk,wqhd->wkhd", d_scores, query, preferred_element_type=jnp.float32
    ).astype(jnp.bfloat16)
    d_qkv = jnp.concatenate(
        [
            d_query.reshape(total_rows, inner),
            d_keys.reshape(total_rows, inner),
            d_values.reshape(total_rows, inner),
        ],
        axis=1,
    )
    return (mixed, d_qkv)


def audio_attend(qkv_rows, out_cot):
    return attend(qkv_rows, out_cot, A_HEADS, A_SIZE, WIN)


def vision_attend(qkv_rows, out_cot):
    return attend(qkv_rows, out_cot, V_HEADS, V_SIZE, VWIN)


def encode(x_rows, cot_rows, w_qkv, w_out, gain, kind_index):
    x_float = x_rows.astype(jnp.float32)
    mean_row = jnp.mean(x_float, axis=-1, keepdims=True)
    centered = x_float - mean_row
    inverse = lax.rsqrt(jnp.mean(centered * centered, axis=-1, keepdims=True) + EPSILON)
    x_hat = centered * inverse
    gain_float = gain.astype(jnp.float32)
    normed = (x_hat * gain_float).astype(jnp.bfloat16)
    qkv_rows = jnp.dot(normed, w_qkv, preferred_element_type=jnp.float32).astype(jnp.bfloat16)
    d_attn = jnp.dot(cot_rows, w_out.T, preferred_element_type=jnp.float32).astype(jnp.bfloat16)
    mixed, d_qkv = lax.cond(kind_index == 0, audio_attend, vision_attend, qkv_rows, d_attn)
    output = (x_float + jnp.dot(mixed, w_out, preferred_element_type=jnp.float32)).astype(
        jnp.bfloat16
    )
    grad_out = jnp.dot(mixed.T, cot_rows, preferred_element_type=jnp.float32)
    grad_qkv = jnp.dot(normed.T, d_qkv, preferred_element_type=jnp.float32)
    d_normed = jnp.dot(d_qkv, w_qkv.T, preferred_element_type=jnp.float32)
    grad_gain = jnp.sum(d_normed * x_hat, axis=0)
    scaled = d_normed * gain_float
    d_input = inverse * (
        scaled
        - jnp.mean(scaled, axis=-1, keepdims=True)
        - x_hat * jnp.mean(scaled * x_hat, axis=-1, keepdims=True)
    )
    input_grad = (cot_rows.astype(jnp.float32) + d_input).astype(jnp.bfloat16)
    return (output, input_grad, grad_qkv, grad_out, grad_gain)


def shards(blocks, cotangent, modality, time_rank, qkv_weight, out_weight, norm_gain):
    block_count, window, width = blocks.shape
    row_count = lax.axis_size("grp")
    slots = row_count * CAP
    one_hot = (modality[:, None] == jnp.arange(2, dtype=jnp.int32)[None, :]).astype(jnp.int32)
    earlier = jnp.cumsum(one_hot, axis=0) - one_hot
    order_in_kind = jnp.sum(earlier * one_hot, axis=1)
    slot_index = modality * 2 * CAP + order_in_kind % 2 * CAP + order_in_kind // 2
    send_blocks = jnp.zeros((slots, window, width), jnp.bfloat16).at[slot_index].set(blocks)
    send_cot = jnp.zeros((slots, window, width), jnp.bfloat16).at[slot_index].set(cotangent)
    recv_blocks, recv_cot = (
        lax.all_to_all(send_blocks, "grp", split_axis=0, concat_axis=0, tiled=True),
        lax.all_to_all(send_cot, "grp", split_axis=0, concat_axis=0, tiled=True),
    )
    kind_index = lax.axis_index("grp") // 2
    local_qkv = lax.dynamic_index_in_dim(qkv_weight, kind_index, 0, keepdims=False)
    local_out = lax.dynamic_index_in_dim(out_weight, kind_index, 0, keepdims=False)
    local_gain = lax.dynamic_index_in_dim(norm_gain, kind_index, 0, keepdims=False)
    w_qkv, w_out, gain = (
        lax.all_gather(local_qkv, "dp", axis=0, tiled=True),
        lax.all_gather(local_out, "dp", axis=0, tiled=True),
        lax.all_gather(local_gain, "dp", axis=0, tiled=True),
    )
    output, input_grad, grad_qkv, grad_out, grad_gain = encode(
        recv_blocks.reshape(slots * window, width),
        recv_cot.reshape(slots * window, width),
        w_qkv,
        w_out,
        gain,
        kind_index,
    )
    back_out, back_grad = (
        lax.all_to_all(
            output.reshape(slots, window, width), "grp", split_axis=0, concat_axis=0, tiled=True
        ),
        lax.all_to_all(
            input_grad.reshape(slots, window, width), "grp", split_axis=0, concat_axis=0, tiled=True
        ),
    )
    encoded = jnp.zeros_like(blocks).at[time_rank].set(back_out[slot_index])
    block_grad = jnp.zeros_like(blocks).at[time_rank].set(back_grad[slot_index])
    other_qkv, other_out, other_gain = (
        from_partner(grad_qkv.astype(jnp.bfloat16), "grp", 0).astype(grad_qkv.dtype),
        from_partner(grad_out.astype(jnp.bfloat16), "grp", 0).astype(grad_out.dtype),
        from_partner(grad_gain.astype(jnp.bfloat16), "grp", 0).astype(grad_gain.dtype),
    )
    share_qkv, share_out, share_gain = (
        lax.psum_scatter(grad_qkv + other_qkv, "dp", scatter_dimension=0, tiled=True),
        lax.psum_scatter(grad_out + other_out, "dp", scatter_dimension=0, tiled=True),
        lax.psum_scatter(grad_gain + other_gain, "dp", scatter_dimension=0, tiled=True),
    )
    return (encoded, block_grad, share_qkv[None], share_out[None], share_gain[None])


def solution(mesh):
    return jax.shard_map(
        shards,
        mesh=mesh,
        in_specs=(
            P(("grp", "dp"), None, None),
            P(("grp", "dp"), None, None),
            P(("grp", "dp")),
            P(("grp", "dp")),
            P(None, "dp", None),
            P(None, "dp", None),
            P(None, "dp"),
        ),
        out_specs=(
            P(("grp", "dp"), None, None),
            P(("grp", "dp"), None, None),
            P("grp", "dp", None),
            P("grp", "dp", None),
            P("grp", "dp"),
        ),
        check_vma=False,
    )
```

profile of v0, /device:TPU:2, one launch (start us, length us, event | category | flops | bytes accessed | tf_op | source)
XLA Modules:
  0.0 632.4 jit_solution(9398446954033330072)
XLA Ops:
  13.7 3.1 scatter_fusion
  16.8 4.8 all-to-all-start
  23.2 3.4 scatter_fusion.1
  26.7 25.3 %all-to-all-done = bf16[8,128,1280]{2,1,0:T(8,128)(2,1)S(1)} async-done(((bf16[8,128,1280]{2,1,0:T(8,128)(2,1)}), bf16[8,128,1280]{2,1,0:T(8,128)(2,1)S(1)}, u32[]{:S(2)}, u32[]{:S(2)}) %all-to-all-start) | async-done | bytes 2621472 | tf_op jit(solution)/shard_map/all_to_all | solution.py:121
  52.0 6.0 all-to-all-start.1
  59.6 67.6 %all-reduce = bf16[1280]{0:T(1024)(128)(2,1)S(1)} all-reduce(bf16[1280]{0:T(1024)(128)(2,1)S(1)} %dynamic-update-slice), channel_id=2, replica_groups=mesh['grp'=4,'dp'=32] {'dp'}, use_global_device_ids=true, to_apply=%add | all-reduce | flops 1280 | bytes 5120
  130.7 6.0 fusion.112
  136.8 9.9 %fusion.106 = bf16[1024,1920]{1,0:T(8,128)(2,1)} fusion(bf16[1024,1280]{1,0:T(8,128)(2,1)} %fusion.94, bf16[1,1280,1920]{2,1,0:T(8,128)(2,1)} %all-gather.6.cloned.1.call-done), kind=kOutput, calls=%fused_computation.114 | convolution fusion | flops 5035130880 | bytes 11468800 | tf_op jit(solution)/shard_map/dot_general | solution.py:90
  146.6 81.0 %conditional.1 = (bf16[1024,640]{1,0:T(8,128)(2,1)}, bf16[1024,1920]{1,0:T(8,128)(2,1)}) conditional(s32[]{:T(128)} %convert_element_type.118, (bf16[1024,1920]{1,0:T(8,128)(2,1)}, bf16[1024,640]{1,0:T(8,128)(2,1)}) %tuple.16, (bf16[1024,1920]{1,0:T(8,128)(2,1)}, bf16[1024,640]{1,0:T(8,128)(2,1)}) %tuple.16), branch_computations={%region_6.10_spmd, %region_10.14_spmd} | conditional | flops 1049907584 | bytes 173220080 | solution.py:92
  150.5 6.3 copy.126
  156.8 3.0 slice_bitcast_fusion.1
  162.7 3.6 fusion.125
  173.5 3.3 fusion.73
  176.8 10.4 %fusion.64 = bf16[8,128,10,64]{1,3,2,0:T(8,128)(2,1)} fusion(f32[8,10,128,128]{2,3,1,0:T(8,128)} %fusion.73, bf16[8,128,10,64]{1,0,3,2:T(8,128)(2,1)} %bitcast.157, f32[8,10,128,128]{2,3,1,0:T(8,128)} %get-tuple-element.65, f32[8,10,128]{2,1,0:T(8,128)S(1)} %get-tuple-element.64), kind=kOutput, calls=%fused_computation.63 | convolution fusion | flops 177612928 | bytes 13148160 | tf_op jit(solution)/shard_map/cond/branch_1_fun/whqk,wqhd->wkhd/dot_general | solution.py:60
  189.6 4.4 fusion.62
  197.2 10.4 %fusion.67 = bf16[8,128,10,64]{1,3,2,0:T(8,128)(2,1)} fusion(f32[8,10,128,128]{2,3,1,0:T(8,128)} %fusion.73, bf16[8,128,10,64]{1,0,3,2:T(8,128)(2,1)} %bitcast.155, f32[8,10,128,128]{2,3,1,0:T(8,128)} %get-tuple-element.65, f32[8,10,128]{2,1,0:T(8,128)S(1)} %get-tuple-element.64), kind=kOutput, calls=%fused_computation.64 | convolution fusion | flops 177612928 | bytes 13148160 | tf_op jit(solution)/shard_map/cond/branch_1_fun/whqk,wkhd->wqhd/dot_general | solution.py:57
  212.7 6.3 copy.125
  218.9 3.7 fusion.63
  227.6 10.6 %fusion.127 = (bf16[1280,1920]{1,0:T(8,128)(2,1)S(1)}, f32[1280,1920]{1,0:T(8,128)}) fusion(bf16[1024,1280]{1,0:T(8,128)(2,1)} %fusion.94, bf16[1024,1920]{1,0:T(8,128)(2,1)} %get-tuple-element.20), kind=kOutput, calls=%fused_computation.152 | convolution fusion | flops 5035622400 | bytes 21299200 | tf_op jit(solution)/shard_map/dot_general | solution.py:97
  238.6 104.4 %collective-permute-done = bf16[1280,1920]{1,0:T(8,128)(2,1)S(1)} collective-permute-done((bf16[1280,1920]{1,0:T(8,128)(2,1)S(1)}, bf16[1280,1920]{1,0:T(8,128)(2,1)S(1)}, u32[]{:S(2)}, u32[]{:S(2)}) %collective-permute-start) | collective-permute-done | bytes 4915232 | tf_op jit(solution)/shard_map/ppermute | solution.py:27
  343.0 8.6 %convert_add_fusion = f32[1280,1920]{1,0:T(8,128)} fusion(f32[1280,1920]{1,0:T(8,128)} %get-tuple-element.75, bf16[1280,1920]{1,0:T(8,128)(2,1)S(1)} %collective-permute-done), kind=kLoop, calls=%fused_computation.89 | loop fusion | flops 4915200 | bytes 24576000 | tf_op jit(solution)/shard_map/add | solution.py:157
  351.7 6.4 %fusion.128 = (bf16[640,1280]{1,0:T(8,128)(2,1)}, f32[640,1280]{1,0:T(8,128)}) fusion(bf16[1024,640]{1,0:T(8,128)(2,1)} %get-tuple-element.19, bf16[1024,1280]{1,0:T(8,128)(2,1)} %bitcast.14), kind=kOutput, calls=%fused_computation.153 | convolution fusion | flops 1678540800 | bytes 8847360 | tf_op jit(solution)/shard_map/dot_general | solution.py:96
  358.3 8.6 %fusion.100 = (f32[1280]{0:T(1024)S(1)}, f32[1024]{0:T(1024)S(1)}, f32[1024]{0:T(1024)S(1)}, f32[1024,1280]{1,0:T(8,128)S(1)}) fusion(bf16[8,128,1280]{2,1,0:T(8,128)(2,1)S(1)} %all-to-all-done, f32[1024]{0:T(1024)S(1)} %rsqrt_bitcast_fusion, f32[1024]{0:T(1024)S(1)} %get-tuple-element.68, f32[1280]{0:T(1024)S(1)} %convert_element_type.135, ...), kind=kOutput, calls=%fused_computation.107 | convolution fusion | flops 5044958208 | bytes 16738304 | tf_op jit(solution)/shard_map/dot_general | solution.py:98
  367.0 4.6 fusion.99
  371.6 39.6 %all-to-all-start.3 = ((bf16[8,128,1280]{2,1,0:T(8,128)(2,1)}), bf16[8,128,1280]{2,1,0:T(8,128)(2,1)}, u32[]{:S(2)}, u32[]{:S(2)}) async-start(bf16[8,128,1280]{2,1,0:T(8,128)(2,1)} %bitcast.145), calls=%async_computation.3 | async-start | bytes 5242880 | tf_op jit(solution)/shard_map/all_to_all | solution.py:145
  411.6 6.6 %fusion.101 = bf16[1024,1280]{1,0:T(8,128)(2,1)} fusion(bf16[8,128,1280]{2,1,0:T(8,128)(2,1)S(1)} %all-to-all-done, bf16[1024,640]{1,0:T(8,128)(2,1)} %get-tuple-element.19, bf16[1,640,1280]{2,0,1:T(2,128)(2,1)} %all-gather.8.cloned.1.call-done), kind=kOutput, calls=%fused_computation.108 | convolution fusion | flops 1681653760 | bytes 8192000 | tf_op jit(solution)/shard_map/dot_general | solution.py:93
  418.2 3.5 convert_add_fusion.1
  421.7 32.7 %all-to-all-done.3 = bf16[8,128,1280]{2,1,0:T(8,128)(2,1)} async-done(((bf16[8,128,1280]{2,1,0:T(8,128)(2,1)}), bf16[8,128,1280]{2,1,0:T(8,128)(2,1)}, u32[]{:S(2)}, u32[]{:S(2)}) %all-to-all-start.3) | async-done | bytes 2621472 | tf_op jit(solution)/shard_map/all_to_all | solution.py:145
  454.4 6.3 %all-to-all-start.2 = ((bf16[8,128,1280]{2,1,0:T(8,128)(2,1)}), bf16[8,128,1280]{2,1,0:T(8,128)(2,1)}, u32[]{:S(2)}, u32[]{:S(2)}) async-start(bf16[8,128,1280]{2,1,0:T(8,128)(2,1)} %bitcast.15), calls=%async_computation.2 | async-start | bytes 5242880 | tf_op jit(solution)/shard_map/all_to_all | solution.py:142
  460.7 77.9 %fusion = f32[24,1280]{1,0:T(8,128)S(1)} fusion(f32[640,1280]{1,0:T(8,128)} %convert_add_fusion.1), kind=kCustom, calls=%all-reduce-scatter | all-reduce-scatter fusion | flops 983041 | bytes 3400192
  547.7 64.6 %all-reduce.3 = f32[1280]{0:T(1024)S(1)} all-reduce(f32[1280]{0:T(1024)S(1)} %convert_add_fusion.2), channel_id=7, replica_groups=mesh['grp'=4,'dp'=32] {'dp'}, use_global_device_ids=true, to_apply=%region_21.22.clone | all-reduce | flops 1280 | bytes 10240
  622.7 2.9 scatter_fusion.2
  (112 shorter events, 57.3 us)
Async XLA Ops:
  7.2 1.9 copy-start
  7.2 6.5 %copy-start.14 = (bf16[4,128,1280]{2,1,0:T(8,128)(2,1)S(1)}, bf16[4,128,1280]{2,1,0:T(8,128)(2,1)}, u32[]{:S(2)}) copy-start(bf16[4,128,1280]{2,1,0:T(8,128)(2,1)} %param.9) | copy-start | bytes 3932164
  7.2 123.5 %all-gather.8.cloned.1.call-start = ((), (), s32[]{:S(2)}) async-start(), calls=%async_computation.6 | async-start | bytes 3379200 | tf_op jit(solution)/shard_map/all_gather | solution.py:130
  9.0 127.7 %all-gather.6.cloned.1.call-start = ((), (), s32[]{:S(2)}) async-start(), calls=%async_computation.5 | async-start | bytes 5068800 | tf_op jit(solution)/shard_map/all_gather | solution.py:129
  12.0 11.3 %copy-start.15 = (s32[4]{0:T(128)}, s32[4]{0:T(128)S(1)}, u32[]{:S(2)}) copy-start(s32[4]{0:T(128)S(1)} %compare_select_fusion) | copy-start | bytes 52
  16.8 35.2 %all-to-all-start = ((bf16[8,128,1280]{2,1,0:T(8,128)(2,1)}), bf16[8,128,1280]{2,1,0:T(8,128)(2,1)S(1)}, u32[]{:S(2)}, u32[]{:S(2)}) async-start(bf16[8,128,1280]{2,1,0:T(8,128)(2,1)} %scatter_fusion), calls=%async_computation | async-start | bytes 5242880 | tf_op jit(solution)/shard_map/all_to_all | solution.py:121
  26.7 31.3 %copy-start.17 = (u32[128]{0:T(128)S(1)}, u32[128]{0:T(128)}, u32[]{:S(2)}) copy-start(u32[128]{0:T(128)} %constant.99) | copy-start | bytes 1540
  26.7 32.6 %copy-start.18 = (bf16[2,40]{1,0:T(2,128)(2,1)S(1)}, bf16[2,40]{1,0:T(2,128)(2,1)}, u32[]{:S(2)}) copy-start(bf16[2,40]{1,0:T(2,128)(2,1)} %param.15) | copy-start | bytes 484
  52.0 78.7 %all-to-all-start.1 = ((bf16[8,128,1280]{2,1,0:T(8,128)(2,1)}), bf16[8,128,1280]{2,1,0:T(8,128)(2,1)}, u32[]{:S(2)}, u32[]{:S(2)}) async-start(bf16[8,128,1280]{2,1,0:T(8,128)(2,1)} %scatter_fusion.1), calls=%async_computation.1 | async-start | bytes 5242880 | tf_op jit(solution)/shard_map/all_to_all | solution.py:122
  58.0 567.6 %reduce-scatter.6.cloned.1.call-start = ((), (), s32[]{:S(2)}) async-start(), calls=%async_computation.7 | async-start | bytes 10137600
  160.2 1.1 copy-start.9
  160.6 1.2 copy-start.8
  170.6 2.9 copy-start.7
  187.2 2.4 copy-start.11
  207.6 2.8 copy-start.5
  207.6 2.8 copy-start.6
  238.2 104.8 %collective-permute-start = (bf16[1280,1920]{1,0:T(8,128)(2,1)S(1)}, bf16[1280,1920]{1,0:T(8,128)(2,1)S(1)}, u32[]{:S(2)}, u32[]{:S(2)}) collective-permute-start(bf16[1280,1920]{1,0:T(8,128)(2,1)S(1)} %get-tuple-element.74), channel_id=1, source_target_pairs={{0,32},{32,0},{64,96},{96,64},{1,33},{33,1},{65,97},{97,65},{2,34}... | collective-permute-start | bytes 14745608 | tf_op jit(solution)/shard_map/ppermute | solution.py:27
  351.6 6.7 %copy-start.13 = (bf16[1024,1920]{1,0:T(8,128)(2,1)S(1)}, bf16[1024,1920]{1,0:T(8,128)(2,1)}, u32[]{:S(2)}) copy-start(bf16[1024,1920]{1,0:T(8,128)(2,1)} %get-tuple-element.20) | copy-start | bytes 11796484
  358.1 60.1 %collective-permute-start.1 = (bf16[640,1280]{1,0:T(8,128)(2,1)}, bf16[640,1280]{1,0:T(8,128)(2,1)}, u32[]{:S(2)}, u32[]{:S(2)}) collective-permute-start(bf16[640,1280]{1,0:T(8,128)(2,1)} %get-tuple-element.76), channel_id=1, source_target_pairs={{0,32},{32,0},{64,96},{96,64},{1,33},{33,1},{65,97},{97,65},{2,34}... | collective-permute-start | bytes 4915208 | tf_op jit(solution)/shard_map/ppermute | solution.py:27
  371.6 39.6 %copy-start.19 = (s32[4]{0:T(128)S(1)}, s32[4]{0:T(128)}, u32[]{:S(2)}) copy-start(s32[4]{0:T(128)} %param.12) | copy-start | bytes 52
  371.6 82.8 %all-to-all-start.3 = ((bf16[8,128,1280]{2,1,0:T(8,128)(2,1)}), bf16[8,128,1280]{2,1,0:T(8,128)(2,1)}, u32[]{:S(2)}, u32[]{:S(2)}) async-start(bf16[8,128,1280]{2,1,0:T(8,128)(2,1)} %bitcast.145), calls=%async_computation.3 | async-start | bytes 5242880 | tf_op jit(solution)/shard_map/all_to_all | solution.py:145
  411.3 6.9 %copy-start.2 = (f32[640,1280]{1,0:T(8,128)S(1)}, f32[640,1280]{1,0:T(8,128)}, u32[]{:S(2)}) copy-start(f32[640,1280]{1,0:T(8,128)} %get-tuple-element.77) | copy-start | bytes 9830404
  411.3 133.7 %collective-permute-start.2 = (bf16[1280]{0:T(1024)(128)(2,1)S(1)}, bf16[1280]{0:T(1024)(128)(2,1)S(1)}, u32[]{:S(2)}, u32[]{:S(2)}) collective-permute-start(bf16[1280]{0:T(1024)(128)(2,1)S(1)} %convert_element_type.131), channel_id=1, source_target_pairs={{0,32},{32,0},{64,96},{96,64},{1,33},{33,1},{65,97},{97,65},{2,34}... | collective-permute-start | bytes 7688 | tf_op jit(solution)/shard_map/ppermute | solution.py:27
  454.4 164.7 %all-to-all-start.2 = ((bf16[8,128,1280]{2,1,0:T(8,128)(2,1)}), bf16[8,128,1280]{2,1,0:T(8,128)(2,1)}, u32[]{:S(2)}, u32[]{:S(2)}) async-start(bf16[8,128,1280]{2,1,0:T(8,128)(2,1)} %bitcast.15), calls=%async_computation.2 | async-start | bytes 5242880 | tf_op jit(solution)/shard_map/all_to_all | solution.py:142
  460.7 79.2 %copy-start.16 = (s32[4]{0:T(128)S(1)}, s32[4]{0:T(128)}, u32[]{:S(2)}) copy-start(s32[4]{0:T(128)} %copy-done.15) | copy-start | bytes 52
  538.6 7.7 %collective-permute-start.8 = (f32[4,1280]{1,0:T(4,128)S(1)}, f32[4,1280]{1,0:T(4,128)S(1)}, u32[]{:S(2)}, u32[]{:S(2)}) collective-permute-start(f32[4,1280]{1,0:T(4,128)S(1)} %slice.25), channel_id=1, source_target_pairs={{0,6},{1,7},{2,8},{3,9},{4,10},{5,11},{6,12},{7,13},{8,14},{9,15},... | collective-permute-start | bytes 61448
  541.1 71.7 %collective-permute-start.3 = (f32[24,1280]{1,0:T(8,128)S(1)}, f32[24,1280]{1,0:T(8,128)S(1)}, u32[]{:S(2)}, u32[]{:S(2)}) collective-permute-start(f32[24,1280]{1,0:T(8,128)S(1)} %fusion), channel_id=1, source_target_pairs={{0,1},{1,2},{2,3},{3,4},{4,5},{5,6},{6,7},{7,8},{8,9},{9,10},{10,1... | collective-permute-start | bytes 368648
  542.4 70.4 %collective-permute-start.4 = (f32[24,1280]{1,0:T(8,128)S(1)}, f32[24,1280]{1,0:T(8,128)S(1)}, u32[]{:S(2)}, u32[]{:S(2)}) collective-permute-start(f32[24,1280]{1,0:T(8,128)S(1)} %fusion), channel_id=1, source_target_pairs={{0,2},{1,3},{2,4},{3,5},{4,6},{5,7},{6,8},{7,9},{8,10},{9,11},{10,... | collective-permute-start | bytes 368648
  543.7 69.1 %collective-permute-start.5 = (f32[24,1280]{1,0:T(8,128)S(1)}, f32[24,1280]{1,0:T(8,128)S(1)}, u32[]{:S(2)}, u32[]{:S(2)}) collective-permute-start(f32[24,1280]{1,0:T(8,128)S(1)} %fusion), channel_id=1, source_target_pairs={{0,3},{1,4},{2,5},{3,6},{4,7},{5,8},{6,9},{7,10},{8,11},{9,12},{10... | collective-permute-start | bytes 368648
  545.1 67.8 %collective-permute-start.6 = (f32[24,1280]{1,0:T(8,128)S(1)}, f32[24,1280]{1,0:T(8,128)S(1)}, u32[]{:S(2)}, u32[]{:S(2)}) collective-permute-start(f32[24,1280]{1,0:T(8,128)S(1)} %fusion), channel_id=1, source_target_pairs={{0,4},{1,5},{2,6},{3,7},{4,8},{5,9},{6,10},{7,11},{8,12},{9,13},{1... | collective-permute-start | bytes 368648
  546.4 66.5 %collective-permute-start.7 = (f32[24,1280]{1,0:T(8,128)S(1)}, f32[24,1280]{1,0:T(8,128)S(1)}, u32[]{:S(2)}, u32[]{:S(2)}) collective-permute-start(f32[24,1280]{1,0:T(8,128)S(1)} %fusion), channel_id=1, source_target_pairs={{0,5},{1,6},{2,7},{3,8},{4,9},{5,10},{6,11},{7,12},{8,13},{9,14},{... | collective-permute-start | bytes 368648
  619.1 6.5 %copy-start.1 = (bf16[2,40,1920]{2,1,0:T(8,128)(2,1)S(1)}, bf16[2,40,1920]{2,1,0:T(8,128)(2,1)}, u32[]{:S(2)}) copy-start(bf16[2,40,1920]{2,1,0:T(8,128)(2,1)} %param.13) | copy-start | bytes 921604
  (2 other events, 2.1 us)
Sparse Core Ops, SparseCore 0:
  10.9 47.8 all-gather.7
  61.7 46.6 all-gather.5
  351.8 125.9 reduce-scatter.5
where the time goes:
time: 640 us; the launch traced here: 632 us
  blocking collectives  210 us (33%)
  waiting for transfers between devices  163 us (25%)
  matrix products  81.2 us (13%)
  starting transfers between devices  65.6 us (10%)
  local copies, waits for them, and re-layouts  64.4 us (10%)
  other arithmetic  28.3 us (4%)
  between operations  16.1 us (3%)
    unnamed x3, blocking collectives  210 us
    ppermute x3, waiting for transfers between devices, from_partner(): return lax.ppermute(block, axis, route)  104 us
    all_to_all x1, starting transfers between devices, shards(): lax.all_to_all(input_grad.reshape(slots, window, width), 'grp', split_axi...  39.6 us
    all_to_all x1, waiting for transfers between devices, shards(): lax.all_to_all(input_grad.reshape(slots, window, width), 'grp', split_axi...  32.7 us
    all_to_all x1, waiting for transfers between devices, shards(): lax.all_to_all(send_blocks, 'grp', split_axis=0, concat_axis=0, tiled=True)  25.3 us
    another operation x8, local copies, waits for them, and re-layouts  22.5 us
  transfers between devices with their start and end apart: 16, of which 3 were waited for; matrix products, arithmetic and copies ran while one was open for 23% of the time, Pallas kernels for 0%

commit v1 on v0

v1 whole, which is shorter than its diff:
```python
import math

import jax
import jax.numpy as jnp
from jax import lax
from jax.experimental import pallas as pl
from jax.experimental.pallas import tpu as pltpu
from jax.sharding import PartitionSpec as P

A_HEADS = 10
A_SIZE = 64
V_HEADS = 8
V_SIZE = 80
WIN = 128
VWIN = 64
LANES = 128
EPSILON = 1e-05
VMEM_BYTES = 60 * 1024 * 1024


def normalized(x):
    mean_row = jnp.mean(x, axis=-1, keepdims=True)
    centered = x - mean_row
    inverse = lax.rsqrt(jnp.mean(centered * centered, axis=-1, keepdims=True) + EPSILON)
    return centered * inverse, inverse


def nt_dot(a, b):
    return lax.dot_general(a, b, (((1,), (1,)), ((), ())), preferred_element_type=jnp.float32)


def tn_dot(a, b):
    return lax.dot_general(a, b, (((0,), (0,)), ((), ())), preferred_element_type=jnp.float32)


def nn_dot(a, b):
    return jnp.dot(a, b, preferred_element_type=jnp.float32)


def attend_pair(query, keys, values, cot, first, second, scale, same_window):
    zero = jnp.zeros((), jnp.bfloat16)

    def stacked(rows):
        return jnp.concatenate(
            [jnp.where(first, rows, zero), jnp.where(second, rows, zero)], axis=0
        )

    query_two = stacked(query)
    cot_two = stacked(cot)
    scores = nt_dot(query_two, keys) * scale
    if same_window is not None:
        scores = jnp.where(same_window, scores, -1e30)
    row_max = jnp.max(scores, axis=-1, keepdims=True)
    exponent = jnp.exp(scores - row_max)
    probs = exponent * (1.0 / jnp.sum(exponent, axis=-1, keepdims=True))
    probs_low = probs.astype(jnp.bfloat16)
    d_probs = nt_dot(cot_two, values)
    inner = jnp.sum(d_probs * probs, axis=-1, keepdims=True)
    d_scores = (probs * (d_probs - inner) * scale).astype(jnp.bfloat16)

    def beside(rows):
        return jnp.concatenate([rows[:WIN], rows[WIN:]], axis=1)

    mixed = nn_dot(beside(probs_low), stacked(values))
    d_values = tn_dot(probs_low, cot_two)
    d_query = nn_dot(beside(d_scores), stacked(keys))
    d_keys = tn_dot(d_scores, query_two)
    return mixed, d_query, d_keys, d_values


def attend_block(heads, size, vision, qkv, cot, out, d_qkv):
    inner = heads * size
    scale = 1.0 / math.sqrt(size)
    same_window = None
    if vision:
        row = lax.broadcasted_iota(jnp.int32, (2 * WIN, WIN), 0)
        col = lax.broadcasted_iota(jnp.int32, (2 * WIN, WIN), 1)
        same_window = (row % WIN) // VWIN == col // VWIN
    tiles = [[None] * (inner // LANES) for _ in range(4)]
    for pair in range(heads // 2):
        low = 2 * pair * size
        start = low // LANES * LANES
        stop = -(-(low + 2 * size) // LANES) * LANES
        lane = lax.broadcasted_iota(jnp.int32, (WIN, stop - start), 1) + start
        first = (lane >= low) & (lane < low + size)
        second = (lane >= low + size) & (lane < low + 2 * size)
        found = attend_pair(
            qkv[:, start:stop],
            qkv[:, inner + start : inner + stop],
            qkv[:, 2 * inner + start : 2 * inner + stop],
            cot[:, start:stop],
            first,
            second,
            scale,
            same_window,
        )
        for which in range(4):
            for tile in range(start // LANES, stop // LANES):
                at = tile * LANES - start
                part = found[which][:, at : at + LANES]
                held = tiles[which][tile]
                tiles[which][tile] = part if held is None else held + part
        done = range(start // LANES, (low + 2 * size) // LANES)
        for tile in done:
            at = slice(tile * LANES, (tile + 1) * LANES)
            out[:, at] = tiles[0][tile].astype(jnp.bfloat16)
            for which in range(3):
                to = slice(which * inner + tile * LANES, which * inner + (tile + 1) * LANES)
                d_qkv[:, to] = tiles[which + 1][tile].astype(jnp.bfloat16)


def encode_kernel(
    kind_ref,
    rank_ref,
    x_ref,
    cot_ref,
    wq_ref,
    wo_ref,
    gain_ref,
    enc_ref,
    grad_ref,
    dwq_ref,
    dwo_ref,
    dgain_ref,
    qkv_s,
    dattn_s,
    mixed_s,
    dqkv_s,
    ht_s,
    mt_s,
):
    blocks = x_ref.shape[0]
    width = x_ref.shape[2]
    inner = wo_ref.shape[1]
    dgain_ref[...] = jnp.zeros_like(dgain_ref)

    @pl.loop(0, blocks)
    def _(b):
        kind = kind_ref[b]
        rank = rank_ref[b]
        x = x_ref[b].astype(jnp.float32)
        x_hat, inverse = normalized(x)
        gain = gain_ref[kind]
        normed = (x_hat * gain).astype(jnp.bfloat16)
        columns = pl.ds(pl.multiple_of(b * WIN, WIN), WIN)
        turned = normed.T
        for m in range(2):
            ht_s[m, :, columns] = jnp.where(kind == m, turned, jnp.zeros_like(turned))
        for at in range(0, 3 * inner, inner):
            qkv_s[:, at : at + inner] = nn_dot(normed, wq_ref[kind, :, at : at + inner]).astype(
                jnp.bfloat16
            )
        cot = cot_ref[b]
        dattn_s[...] = nt_dot(cot, wo_ref[kind]).astype(jnp.bfloat16)
        d_qkv = dqkv_s.at[b]

        @pl.when(kind == 0)
        def _():
            attend_block(A_HEADS, A_SIZE, False, qkv_s, dattn_s, mixed_s, d_qkv)

        @pl.when(kind != 0)
        def _():
            attend_block(V_HEADS, V_SIZE, True, qkv_s, dattn_s, mixed_s, d_qkv)

        mixed = mixed_s[...]
        mixed_t = mixed.T
        for m in range(2):
            mt_s[m, :, columns] = jnp.where(kind == m, mixed_t, jnp.zeros_like(mixed_t))
        enc_ref[rank] = (x + nn_dot(mixed, wo_ref[kind])).astype(jnp.bfloat16)
        d_normed = nt_dot(dqkv_s[b], wq_ref[kind])
        dgain_ref[kind] += jnp.sum(d_normed * x_hat, axis=0, keepdims=True)
        scaled = d_normed * gain
        d_input = inverse * (
            scaled
            - jnp.mean(scaled, axis=-1, keepdims=True)
            - x_hat * jnp.mean(scaled * x_hat, axis=-1, keepdims=True)
        )
        grad_ref[rank] = (cot.astype(jnp.float32) + d_input).astype(jnp.bfloat16)

    cot_all = cot_ref[...].reshape(blocks * WIN, width)
    d_qkv_all = dqkv_s[...].reshape(blocks * WIN, 3 * inner)

    @pl.loop(0, 2)
    def _(m):
        @pl.loop(0, width, step=256)
        def _(r):
            rows = pl.ds(pl.multiple_of(r, 256), 256)
            dwq_ref[m, rows, :] = nn_dot(ht_s[m, rows, :], d_qkv_all).astype(jnp.bfloat16)

        @pl.loop(0, inner, step=128)
        def _(r):
            rows = pl.ds(pl.multiple_of(r, 128), 128)
            dwo_ref[m, rows, :] = nn_dot(mt_s[m, rows, :], cot_all).astype(jnp.bfloat16)


def encode_own(kind, rank, blocks, cotangent, w_qkv, w_out, gain):
    count, window, width = blocks.shape
    inner = w_out.shape[1]
    tokens = count * window
    bf16, f32 = jnp.bfloat16, jnp.float32
    return pl.pallas_call(
        encode_kernel,
        out_shape=(
            jax.ShapeDtypeStruct(blocks.shape, bf16),
            jax.ShapeDtypeStruct(blocks.shape, bf16),
            jax.ShapeDtypeStruct(w_qkv.shape, bf16),
            jax.ShapeDtypeStruct(w_out.shape, bf16),
            jax.ShapeDtypeStruct((2, 1, width), f32),
        ),
        in_specs=[pl.BlockSpec(memory_space=pltpu.SMEM)] * 2
        + [pl.BlockSpec(memory_space=pltpu.VMEM)] * 5,
        out_specs=(pl.BlockSpec(memory_space=pltpu.VMEM),) * 5,
        scratch_shapes=[
            pltpu.VMEM((window, 3 * inner), bf16),
            pltpu.VMEM((window, inner), bf16),
            pltpu.VMEM((window, inner), bf16),
            pltpu.VMEM((count, window, 3 * inner), bf16),
            pltpu.VMEM((2, width, tokens), bf16),
            pltpu.VMEM((2, inner, tokens), bf16),
        ],
        compiler_params=pltpu.CompilerParams(vmem_limit_bytes=VMEM_BYTES),
    )(kind, rank, blocks, cotangent, w_qkv, w_out, gain.astype(f32)[:, None, :])


def shards(blocks, cotangent, modality, time_rank, qkv_weight, out_weight, norm_gain):
    w_qkv = lax.all_gather(qkv_weight, "dp", axis=1, tiled=True)
    w_out = lax.all_gather(out_weight, "dp", axis=1, tiled=True)
    gain = lax.all_gather(norm_gain, "dp", axis=1, tiled=True)
    encoded, block_grad, d_qkv, d_out, d_gain = encode_own(
        modality, time_rank, blocks, cotangent, w_qkv, w_out, gain
    )
    kind = lax.axis_index("grp") // 2

    def shared(grad):
        part = lax.psum_scatter(grad.astype(jnp.float32), "dp", scatter_dimension=1, tiled=True)
        return lax.dynamic_index_in_dim(lax.psum(part, "grp"), kind, 0, keepdims=True)

    return (encoded, block_grad, shared(d_qkv), shared(d_out), shared(d_gain[:, 0, :]))


def solution(mesh):
    return jax.shard_map(
        shards,
        mesh=mesh,
        in_specs=(
            P(("grp", "dp"), None, None),
            P(("grp", "dp"), None, None),
            P(("grp", "dp")),
            P(("grp", "dp")),
            P(None, "dp", None),
            P(None, "dp", None),
            P(None, "dp"),
        ),
        out_specs=(
            P(("grp", "dp"), None, None),
            P(("grp", "dp"), None, None),
            P("grp", "dp", None),
            P("grp", "dp", None),
            P("grp", "dp"),
        ),
        check_vma=False,
    )
```

time: 640 us -> 561 us (0.88)
  waiting for transfers between devices: 163 us -> 310 us
  matrix products: 81.2 us -> 0 us
  starting transfers between devices: 65.6 us -> 0.2 us
  blocking collectives: 210 us -> 156 us
  Pallas kernels: 0 us -> 45.6 us
  local copies, waits for them, and re-layouts: 64.4 us -> 19.5 us
  other arithmetic: 28.3 us -> 12.2 us
    reduce_scatter x0 -> x1, waiting for transfers between devices: none -> 127 us  [shared(): lax.psum_scatter(grad.astype(jnp.float32), 'dp', scatter_dimension=1, til...]
    ppermute x3 -> x0, waiting for transfers between devices: 104 us -> none  [from_partner(): return lax.ppermute(block, axis, route)]
    unnamed x10 -> x6, waiting for transfers between devices: 0.07 us -> 103 us
    unnamed x3 -> x1, blocking collectives: 210 us -> 125 us
    dot_general x12 -> x0, matrix products: 81.2 us -> none  [the longest x1 10.6 us: encode(): grad_qkv = jnp.dot(normed.T, d_qkv, preferred_element_type=jnp.float32)]
    all_gather x2, waiting for transfers between devices: 0.01 us -> 79.9 us  [the longest x1 54 us: shards(): w_qkv = lax.all_gather(qkv_weight, 'dp', axis=1, tiled=True)]
    all_to_all x4 -> x0, waiting for transfers between devices: 58.1 us -> none  [the longest x1 32.7 us: shards(): lax.all_to_all(input_grad.reshape(slots, window, width), 'grp', split_axi...]
    all_to_all x4 -> x0, starting transfers between devices: 56.7 us -> none  [the longest x1 39.6 us: shards(): lax.all_to_all(input_grad.reshape(slots, window, width), 'grp', split_axi...]
  transfers between devices with their start and end apart: 16 -> 5, of which waited for: 3 -> 4; matrix products, arithmetic and copies ran while one was open for 23% -> 4% of each run, Pallas kernels for 0% -> 0%
where the time goes in v1:
time: 561 us; the launch traced here: 559 us
  waiting for transfers between devices  310 us (55%)
  blocking collectives  156 us (28%)
  Pallas kernels  45.6 us (8%)
  local copies, waits for them, and re-layouts  19.5 us (3%)
  between operations  15.1 us (3%)
  other arithmetic  12.2 us (2%)
    reduce_scatter x1, waiting for transfers between devices, shared(): lax.psum_scatter(grad.astype(jnp.float32), 'dp', scatter_dimension=1, til...  127 us
    unnamed x1, blocking collectives  125 us
    unnamed x6, waiting for transfers between devices  103 us
    all_gather x1, waiting for transfers between devices, shards(): w_qkv = lax.all_gather(qkv_weight, 'dp', axis=1, tiled=True)  54 us
    pallas_call x1, Pallas kernels, encode_own(): pl.pallas_call(encode_kernel, out_shape=(jax.ShapeDtypeStruct(blocks.shap...  45.6 us
    all_gather x1, waiting for transfers between devices, shards(): w_out = lax.all_gather(out_weight, 'dp', axis=1, tiled=True)  25.9 us
    all_gather x1, blocking collectives, shards(): gain = lax.all_gather(norm_gain, 'dp', axis=1, tiled=True)  22.9 us
    convert_element_type x1, other arithmetic, shared(): grad.astype(jnp.float32)  12.2 us
  transfers between devices with their start and end apart: 5, of which 4 were waited for; matrix products, arithmetic and copies ran while one was open for 4% of the time, Pallas kernels for 0%

profile of v1, /device:TPU:2, one launch (start us, length us, event | category | flops | bytes accessed | tf_op | source)
XLA Modules:
  0.0 559.0 jit_solution(4775323299204254607)
XLA Ops:
  7.2 0.0 all-gather.6.cloned.1.call-start
  7.2 0.7 all-gather.6.cloned.1.call-update
  7.9 0.0 all-gather.4.cloned.1.call-start
  7.9 0.7 all-gather.4.cloned.1.call-update
  8.6 0.0 all-reduce.6.cloned.1.call-start
  8.7 22.9 %all-gather = bf16[32,40,2]{1,2,0:T(2,128)(2,1)S(1)} all-gather(bf16[1,40,2]{1,2,0:T(2,128)(2,1)} %bitcast.14), channel_id=1, replica_groups=mesh['grp'=4,'dp'=32] {'dp'}, dimensions={0}, use_global_device_ids=true | all-gather | bytes 5280 | tf_op jit(solution)/shard_map/all_gather | solution.py:228
  31.6 0.1 reshape.13
  31.7 0.6 reshape.10.gain_ref
  32.3 25.9 %all-gather.6.cloned.1.call-done = bf16[2,640,1280]{2,0,1:T(2,128)(2,1)} async-done(((bf16[2,20,1280]{2,0,1:T(2,128)(2,1)}), bf16[2,640,1280]{2,0,1:T(2,128)(2,1)}) %all-gather.6.cloned.1.call-update) | async-done | bytes 3276816 | tf_op jit(solution)/shard_map/all_gather | solution.py:227
  58.2 4.1 copy.19.wo_ref
  62.3 54.0 %all-gather.4.cloned.1.call-done.wq_ref = bf16[2,1280,1920]{2,1,0:T(8,128)(2,1)} async-done(((bf16[2,40,1920]{2,1,0:T(8,128)(2,1)}), bf16[2,1280,1920]{2,1,0:T(8,128)(2,1)}) %all-gather.4.cloned.1.call-update) | async-done | bytes 9830416 | tf_op jit(solution)/shard_map/all_gather | solution.py:226
  116.3 45.6 %shard_map.110 = (bf16[4,128,1280]{2,1,0:T(8,128)(2,1)}, bf16[4,128,1280]{2,1,0:T(8,128)(2,1)}, bf16[2,1280,1920]{2,1,0:T(8,128)(2,1)}, bf16[2,640,1280]{2,1,0:T(8,128)(2,1)}, f32[2,1,1280]{2,1,0:T(1,128)}) custom-call(s32[4]{0:T(128)} %kind_ref.1, s32[4]{0:T(128)} %rank_ref.1, bf16[4,128,1280]{2,1,0:T(8,128)(2,1)} %x_ref.1, bf16[4,128,1280]{2,1,0:T(8,128)(2,1)} %cot_ref.1, ...), custom_call_target="tpu_custom_call" | custom-call | tf_op jit(solution)/shard_map/pallas_call | solution.py:201
  162.0 8.0 %copy.20 = f32[2,640,1280]{2,0,1:T(2,128)} copy(bf16[2,640,1280]{2,1,0:T(8,128)(2,1)} %get-tuple-element.13) | data formatting | bytes 9830400 | tf_op jit(solution)/shard_map/convert_element_type | solution.py:235
  170.0 0.0 all-reduce.6.cloned.1.call-update
  170.0 0.0 reduce-scatter.3.cloned.1.call-start
  170.0 12.2 %convert_element_type.7 = f32[2,1280,1920]{2,1,0:T(8,128)} convert(bf16[2,1280,1920]{2,1,0:T(8,128)(2,1)} %get-tuple-element.12) | non-fusion elementwise | flops 4915200 | bytes 29491200 | tf_op jit(solution)/shard_map/convert_element_type | solution.py:235
  182.2 0.0 copy-start.1
  182.2 0.0 reduce-scatter.3.cloned.1.call-update
  182.3 0.0 all-reduce.8.cloned.1.call-start
  182.3 0.6 copy-done.1
  182.9 0.6 dynamic-slice
  184.1 101.7 %all-reduce.6.cloned.1.call-done = f32[2,640,1280]{2,0,1:T(2,128)} async-done(((f32[2,640,1280]{2,0,1:T(2,128)}), f32[2,640,1280]{2,0,1:T(2,128)}) %all-reduce.6.cloned.1.call-update) | async-done | bytes 6553616
  285.8 1.6 constant_dynamic-slice_fusion.1
  287.4 127.0 %reduce-scatter.3.cloned.1.call-done = f32[2,40,1920]{2,1,0:T(8,128)} async-done(((f32[2,1280,1920]{2,1,0:T(8,128)}), f32[2,40,1920]{2,1,0:T(8,128)}) %reduce-scatter.3.cloned.1.call-update) | async-done | bytes 614416 | tf_op jit(solution)/shard_map/reduce_scatter | solution.py:235
  414.4 0.0 all-reduce.8.cloned.1.call-update
  415.1 0.0 copy-done
  415.1 124.8 %all-reduce.1 = f32[2,1280]{1,0:T(2,128)S(1)} all-reduce(f32[2,1280]{1,0:T(2,128)S(1)} %bitcast.12), channel_id=4, replica_groups=mesh['grp'=4,'dp'=32] {'dp'}, use_global_device_ids=true, to_apply=%region_4.5.clone | all-reduce | flops 2560 | bytes 20480
  539.9 0.1 constant_dynamic-slice_fusion
  540.0 8.6 %psum.23 = f32[2,40]{1,0:T(2,128)S(1)} all-reduce(f32[2,40]{1,0:T(2,128)S(1)} %constant_dynamic-slice_fusion), channel_id=1, replica_groups=mesh['grp'=4,'dp'=32] {'grp'}, use_global_device_ids=true, to_apply=%region_5.6 | all-reduce | flops 80 | bytes 640 | tf_op jit(solution)/shard_map/psum | solution.py:236
  548.6 0.5 constant_dynamic-slice_fusion.2
  549.1 1.7 constant_dynamic-slice_fusion.4
  550.8 1.7 constant_dynamic-slice_fusion.3
  (4 shorter events, 0.0 us)
Async XLA Ops:
  7.2 51.1 %all-gather.6.cloned.1.call-start = ((), (), s32[]{:S(2)}) async-start(), calls=%async_computation.2 | async-start | bytes 3379200 | tf_op jit(solution)/shard_map/all_gather | solution.py:227
  7.9 108.4 %all-gather.4.cloned.1.call-start = ((), (), s32[]{:S(2)}) async-start(), calls=%async_computation.1 | async-start | bytes 10137600 | tf_op jit(solution)/shard_map/all_gather | solution.py:226
  8.6 277.1 %all-reduce.6.cloned.1.call-start = ((), (), s32[]{:S(2)}) async-start(), calls=%async_computation.4 | async-start | bytes 13107200
  170.0 244.4 %reduce-scatter.3.cloned.1.call-start = ((), (), s32[]{:S(2)}) async-start(), calls=%async_computation.3 | async-start | bytes 20275200 | tf_op jit(solution)/shard_map/reduce_scatter | solution.py:235
  182.2 0.7 copy-start.1
  182.2 232.8 %copy-start = (f32[2,1,1280]{2,1,0:T(1,128)S(1)}, f32[2,1,1280]{2,1,0:T(1,128)}, u32[]{:S(2)}) copy-start(f32[2,1,1280]{2,1,0:T(1,128)} %get-tuple-element.14) | copy-start | bytes 30724
  182.3 366.8 %all-reduce.8.cloned.1.call-start = ((), (), s32[]{:S(2)}) async-start(), calls=%async_computation.5 | async-start | bytes 1638400 | tf_op jit(solution)/shard_map/psum | solution.py:236
Sparse Core Ops, SparseCore 0:
  10.3 47.8 all-gather.5
  60.6 55.6 all-gather.3
  170.1 115.6 all-reduce.5
  290.2 124.1 reduce-scatter.2
  417.3 43.1 all-reduce.7

commit v2 on v1

--- a/solution.py
+++ b/solution.py
@@ -16,6 +16,9 @@
 LANES = 128
 EPSILON = 1e-05
 VMEM_BYTES = 60 * 1024 * 1024
+RING = 4
+STEPS = 12
+MESH = pl.DeviceIdType.MESH
 
 
 def normalized(x):
@@ -115,12 +118,13 @@
     x_ref,
     cot_ref,
     wq_ref,
-    wo_ref,
-    gain_ref,
+    packed_ref,
     enc_ref,
     grad_ref,
     dwq_ref,
-    dwo_ref,
+    dpacked_ref,
+    wo_ref,
+    gain_ref,
     dgain_ref,
     qkv_s,
     dattn_s,
@@ -132,7 +136,20 @@
     blocks = x_ref.shape[0]
     width = x_ref.shape[2]
     inner = wo_ref.shape[1]
+    count, padded = packed_ref.shape[1:3]
+    rows = inner // count
     dgain_ref[...] = jnp.zeros_like(dgain_ref)
+
+    @pl.loop(0, 2)
+    def _(m):
+        for at in range(0, count, 4):
+            four = [packed_ref[m, at + j, 0:rows].astype(jnp.float32) for j in range(4)]
+            wo_ref[m, at * rows : (at + 4) * rows] = jnp.concatenate(four, axis=0).astype(
+                jnp.bfloat16
+            )
+        gain_ref[m] = sum(
+            packed_ref[m, at, rows : rows + 1].astype(jnp.float32) for at in range(count)
+        )
 
     @pl.loop(0, blocks)
     def _(b):
@@ -187,15 +204,19 @@
             rows = pl.ds(pl.multiple_of(r, 256), 256)
             dwq_ref[m, rows, :] = nn_dot(ht_s[m, rows, :], d_qkv_all).astype(jnp.bfloat16)
 
-        @pl.loop(0, inner, step=128)
-        def _(r):
-            rows = pl.ds(pl.multiple_of(r, 128), 128)
-            dwo_ref[m, rows, :] = nn_dot(mt_s[m, rows, :], cot_all).astype(jnp.bfloat16)
-
-
-def encode_own(kind, rank, blocks, cotangent, w_qkv, w_out, gain):
+        below = jnp.concatenate(
+            [dgain_ref[m], jnp.zeros((padded - rows - 1, width), jnp.float32)], axis=0
+        )
+        for at in range(0, count, 8):
+            eight = nn_dot(mt_s[m, at * rows : (at + 8) * rows, :], cot_all)
+            for j in range(8):
+                one = jnp.concatenate([eight[j * rows : (j + 1) * rows], below], axis=0)
+                dpacked_ref[m, at + j] = one.astype(jnp.bfloat16)
+
+
+def encode_own(kind, rank, blocks, cotangent, w_qkv, packed):
     count, window, width = blocks.shape
-    inner = w_out.shape[1]
+    inner = w_qkv.shape[2] // 3
     tokens = count * window
     bf16, f32 = jnp.bfloat16, jnp.float32
     return pl.pallas_call(
@@ -204,13 +225,15 @@
             jax.ShapeDtypeStruct(blocks.shape, bf16),
             jax.ShapeDtypeStruct(blocks.shape, bf16),
             jax.ShapeDtypeStruct(w_qkv.shape, bf16),
-            jax.ShapeDtypeStruct(w_out.shape, bf16),
-            jax.ShapeDtypeStruct((2, 1, width), f32),
+            jax.ShapeDtypeStruct(packed.shape, bf16),
         ),
         in_specs=[pl.BlockSpec(memory_space=pltpu.SMEM)] * 2
-        + [pl.BlockSpec(memory_space=pltpu.VMEM)] * 5,
-        out_specs=(pl.BlockSpec(memory_space=pltpu.VMEM),) * 5,
+        + [pl.BlockSpec(memory_space=pltpu.VMEM)] * 4,
+        out_specs=(pl.BlockSpec(memory_space=pltpu.VMEM),) * 4,
         scratch_shapes=[
+            pltpu.VMEM((2, inner, width), bf16),
+            pltpu.VMEM((2, 1, width), f32),
+            pltpu.VMEM((2, 1, width), f32),
             pltpu.VMEM((window, 3 * inner), bf16),
             pltpu.VMEM((window, inner), bf16),
             pltpu.VMEM((window, inner), bf16),
@@ -219,23 +242,354 @@
             pltpu.VMEM((2, inner, tokens), bf16),
         ],
         compiler_params=pltpu.CompilerParams(vmem_limit_bytes=VMEM_BYTES),
-    )(kind, rank, blocks, cotangent, w_qkv, w_out, gain.astype(f32)[:, None, :])
+    )(kind, rank, blocks, cotangent, w_qkv, packed)
+
+
+def place_of(index):
+    return index // (2 * RING), index // 2 % RING, index % 2
+
+
+def device_at(y, z, core):
+    return (lax.axis_index("grp"), (y * RING + z) * 2 + core)
+
+
+def step_on(position, by):
+    return lax.rem(position + by + RING, RING)
+
+
+def meet(peers):
+    barrier = pltpu.get_barrier_semaphore()
+    for peer in peers:
+        pl.semaphore_signal(barrier, inc=1, device_id=peer, device_id_type=MESH)
+    pl.semaphore_wait(barrier, len(peers))
+
+
+def gather_kernel(wq_in, wo_in, wq, wo, send_sem, recv_sem, own_sem):
+    y, z, core = place_of(lax.axis_index("dp"))
+    sibling = device_at(y, z, 1 - core)
+    meet(
+        [device_at(step_on(y, by), z, core) for by in (1, -1)]
+        + [device_at(y, step_on(z, by), core) for by in (1, -1)]
+        + [sibling]
+    )
+    sent = []
+
+    class Half:
+        def __init__(self, number, kind, source, target, cut):
+            self.base = number * STEPS
+            self.kind, self.source, self.target, self.cut = kind, source, target, cut
+            self.first, self.second = (y, z) if kind == 0 else (z, y)
+
+        def to(self, first_by, second_by):
+            first, second = step_on(self.first, first_by), step_on(self.second, second_by)
+            return device_at(first, second, core) if self.kind == 0 else device_at(second, first, core)
+
+        def slot(self, first_by):
+            first = step_on(self.first, first_by)
+            if self.kind == 0:
+                return self.target.at[0, first, self.second, core]
+            return self.target.at[1, self.second, first, core]
+
+        def half_slot(self, first_by, upper):
+            size = self.target.shape[-1] - self.cut if upper else self.cut
+            low = self.cut if upper else 0
+            first = step_on(self.first, first_by)
+            if self.kind == 0:
+                return self.target.at[0, first, self.second, core, :, pl.ds(low, size)]
+            return self.target.at[1, self.second, first, core, :, pl.ds(low, size)]
+
+        def ring(self, second_by, part=slice(0, RING), at_core=None):
+            second = step_on(self.second, second_by)
+            at_core = core if at_core is None else at_core
+            if self.kind == 0:
+                return self.target.at[0, part, second, at_core]
+            return self.target.at[1, second, part, at_core]
+
+        def copy(self, number, source, target, device):
+            return pltpu.make_async_remote_copy(
+                src_ref=source,
+                dst_ref=target,
+                send_sem=send_sem.at[self.base + number],
+                recv_sem=recv_sem.at[self.base + number],
+                device_id=device,
+                device_id_type=MESH,
+            )
+
+        def send(self, number, view, device, source=None):
+            one = self.copy(number, view if source is None else source, view, device)
+            one.start()
+            sent.append(one)
+
+        def arrive(self, number, view):
+            self.copy(number, view, view, sibling).wait_recv()
+
+    halves = []
+    for source, target, cut in ((wo_in, wo, wo.shape[-1] // 2), (wq_in, wq, 1024)):
+        for kind in range(2):
+            halves.append(Half(len(halves), kind, source, target, cut))
+    own = []
+    for number, half in enumerate(halves):
+        mine = half.source.at[half.kind]
+        half.send(0, half.slot(0), half.to(1, 0), mine)
+        half.send(1, half.slot(0), half.to(-1, 0), mine)
+        kept = pltpu.make_async_copy(mine, half.slot(0), own_sem.at[number])
+        kept.start()
+        own.append(kept)
+    for half in halves:
+        half.arrive(0, half.slot(-1))
+        half.send(2, half.half_slot(-1, False), half.to(1, 0))
+        half.arrive(1, half.slot(1))
+        half.send(3, half.half_slot(1, True), half.to(-1, 0))
+    low, high = slice(0, RING // 2), slice(RING // 2, RING)
+    for half, kept in zip(halves, own):
+        half.arrive(2, half.half_slot(2, False))
+        half.arrive(3, half.half_slot(2, True))
+        kept.wait()
+        half.send(4, half.ring(0), half.to(0, 1))
+        half.send(5, half.ring(0), half.to(0, -1))
+        half.send(6, half.ring(0), sibling)
+    for half in halves:
+        half.arrive(4, half.ring(-1))
+        half.send(7, half.ring(-1, low), half.to(0, 1))
+        half.send(8, half.ring(-1), sibling)
+        half.arrive(5, half.ring(1))
+        half.send(9, half.ring(1, high), half.to(0, -1))
+        half.send(10, half.ring(1), sibling)
+    for half in halves:
+        half.arrive(7, half.ring(2, low))
+        half.arrive(9, half.ring(2, high))
+        half.send(11, half.ring(2), sibling)
+    for half in halves:
+        for number, by in ((6, 0), (8, -1), (10, 1), (11, 2)):
+            half.arrive(number, half.ring(by, at_core=1 - core))
+    for one in sent:
+        one.wait_send()
+
+
+def gather_weights(qkv_weight, packed):
+    anywhere = pl.BlockSpec(memory_space=pl.ANY)
+    shape = (2, RING, RING, 2)
+    return pl.pallas_call(
+        gather_kernel,
+        out_shape=(
+            jax.ShapeDtypeStruct(shape + qkv_weight.shape[1:], jnp.bfloat16),
+            jax.ShapeDtypeStruct(shape + packed.shape[1:], jnp.bfloat16),
+        ),
+        in_specs=[anywhere] * 2,
+        out_specs=(anywhere,) * 2,
+        scratch_shapes=[
+            pltpu.SemaphoreType.DMA((4 * STEPS,)),
+            pltpu.SemaphoreType.DMA((4 * STEPS,)),
+            pltpu.SemaphoreType.DMA((4,)),
+        ],
+        compiler_params=pltpu.CompilerParams(collective_id=0, has_side_effects=True),
+    )(qkv_weight, packed)
+
+
+def scatter_kernel(
+    dq, do, out_q, out_o, sum_q, sum_o, one_q, one_o, two_q, two_o, three_q, three_o, four_q, four_o,
+    row_q, row_o, send_sem, recv_sem,
+):
+    row = lax.axis_index("grp")
+    index = lax.axis_index("dp")
+    y, z, core = place_of(index)
+    sibling = device_at(y, z, 1 - core)
+    across, beside = (RING - 1 - row, index), (row + 1 - 2 * (row % 2), index)
+    meet(
+        [device_at(step_on(y, by), z, core) for by in (1, -1)]
+        + [device_at(y, step_on(z, by), core) for by in (1, -1)]
+        + [sibling, across, beside]
+    )
+    sent = []
+
+    def copy(number, source, target, device):
+        return pltpu.make_async_remote_copy(
+            src_ref=source,
+            dst_ref=target,
+            send_sem=send_sem.at[number],
+            recv_sem=recv_sem.at[number],
+            device_id=device,
+            device_id_type=MESH,
+        )
+
+    def add(target, *terms):
+        @pl.loop(0, target.shape[0])
+        def _(i):
+            total = target[i].astype(jnp.float32)
+            for term in terms:
+                total = total + term[i].astype(jnp.float32)
+            target[i] = total.astype(jnp.bfloat16)
+
+    class Half:
+        def __init__(self, number, kind, source, total, held, cut):
+            self.base = number * STEPS
+            self.kind, self.source, self.cut = kind, source, cut
+            self.total = total.at[kind]
+            self.held = [one.at[kind] for one in held]
+            self.first, self.second = (y, z) if kind == 0 else (z, y)
+
+        def to(self, first_by, second_by):
+            first, second = step_on(self.first, first_by), step_on(self.second, second_by)
+            return device_at(first, second, core) if self.kind == 0 else device_at(second, first, core)
+
+        def given(self, by, at_core):
+            second = step_on(self.second, by)
+            if self.kind == 0:
+                return self.source.at[0, :, second, at_core]
+            return self.source.at[1, second, :, at_core]
+
+        def ring(self, by):
+            return self.total.at[step_on(self.second, by)]
+
+        def pair(self, by, upper):
+            return self.total.at[step_on(self.second, by), pl.ds(2 * upper, 2)]
+
+        def one(self, by):
+            return self.total.at[self.second, pl.ds(step_on(self.first, by), 1)]
+
+        def part(self, ref, upper):
+            low = self.cut if upper else 0
+            size = ref.shape[-1] - self.cut if upper else self.cut
+            return ref.at[:, :, pl.ds(low, size)]
+
+        def send(self, number, source, target, device):
+            made = copy(self.base + number, source, target, device)
+            made.start()
+            sent.append(made)
+
+        def arrive(self, number, target):
+            copy(self.base + number, target, target, sibling).wait_recv()
+
+    arrays = (
+        (do, sum_o, (one_o, two_o, three_o, four_o), do.shape[-1] // 2),
+        (dq, sum_q, (one_q, two_q, three_q, four_q), 1024),
+    )
+    halves = []
+    for source, total, held, cut in arrays:
+        for kind in range(2):
+            halves.append(Half(len(halves), kind, source, total, held, cut))
+    order = (2, 1, -1, 0)
+    for number, by in enumerate(order):
+        for half in halves:
+            half.send(number, half.given(by, 1 - core), half.ring(by), sibling)
+
+    def take(half, number):
+        by = order[number]
+        half.arrive(number, half.ring(by))
+        add(half.ring(by), half.given(by, core))
+
+    for half in halves:
+        one = half.held[0]
+        take(half, 0)
+        half.send(4, half.pair(2, 0), one.at[0], half.to(0, 1))
+        half.send(5, half.pair(2, 1), one.at[1], half.to(0, -1))
+    for half in halves:
+        one, two = half.held[:2]
+        take(half, 1)
+        half.arrive(4, one.at[0])
+        add(half.pair(1, 0), one.at[0])
+        half.send(6, half.ring(1), two.at[0], half.to(0, 1))
+        take(half, 2)
+        half.arrive(5, one.at[1])
+        add(half.pair(-1, 1), one.at[1])
+        half.send(7, half.ring(-1), two.at[1], half.to(0, -1))
+    for half in halves:
+        take(half, 3)
+    for half in halves:
+        two, three = half.held[1:3]
+        half.arrive(6, two.at[0])
+        half.arrive(7, two.at[1])
+        add(half.ring(0), two.at[0], two.at[1])
+        half.send(8, half.part(half.one(2), 0), half.part(three, 0), half.to(1, 0))
+        half.send(9, half.part(half.one(2), 1), half.part(three, 1), half.to(-1, 0))
+    for half in halves:
+        three, four = half.held[2:]
+        half.arrive(8, half.part(three, 0))
+        add(half.part(half.one(1), 0), half.part(three, 0))
+        half.send(10, half.one(1), four.at[0], half.to(1, 0))
+        half.arrive(9, half.part(three, 1))
+        add(half.part(half.one(-1), 1), half.part(three, 1))
+        half.send(11, half.one(-1), four.at[1], half.to(-1, 0))
+    for half in halves:
+        four = half.held[3]
+        half.arrive(10, four.at[0])
+        half.arrive(11, four.at[1])
+        add(half.one(0), four.at[0], four.at[1])
+
+    kind = row // 2
+    rows = ((sum_o, row_o, out_o, 4 * STEPS), (sum_q, row_q, out_q, 4 * STEPS + 2))
+
+    def own(total, which):
+        first = y + (z - y) * which
+        second = z + (y - z) * which
+        return total.at[which, second, first]
+
+    for total, held, out, number in rows:
+        made = copy(number, own(total, 1 - kind), held.at[0], across)
+        made.start()
+        sent.append(made)
+    for total, held, out, number in rows:
+        copy(number, held.at[0], held.at[0], sibling).wait_recv()
+        mine = own(total, kind)[...].astype(jnp.float32) + held[0].astype(jnp.float32)
+        out[...] = mine
+        held[1] = mine.astype(jnp.bfloat16)
+        made = copy(number + 1, held.at[1], held.at[2], beside)
+        made.start()
+        sent.append(made)
+    for total, held, out, number in rows:
+        copy(number + 1, held.at[2], held.at[2], sibling).wait_recv()
+        out[...] += held[2].astype(jnp.float32)
+    for made in sent:
+        made.wait_send()
+
+
+def scatter_grads(d_qkv, d_packed):
+    bf16, f32 = jnp.bfloat16, jnp.float32
+    q, o = d_qkv.shape[-2:], d_packed.shape[-2:]
+    scratch = []
+    for lead in ((2, RING, RING), (2, 2, 2), (2, 2, RING), (2, 1), (2, 2, 1), (3,)):
+        scratch += [pltpu.VMEM(lead + q, bf16), pltpu.VMEM(lead + o, bf16)]
+    vmem = pl.BlockSpec(memory_space=pltpu.VMEM)
+    return pl.pallas_call(
+        scatter_kernel,
+        out_shape=(jax.ShapeDtypeStruct(q, f32), jax.ShapeDtypeStruct(o, f32)),
+        in_specs=[vmem] * 2,
+        out_specs=(vmem,) * 2,
+        scratch_shapes=scratch
+        + [pltpu.SemaphoreType.DMA((4 * STEPS + 4,)), pltpu.SemaphoreType.DMA((4 * STEPS + 4,))],
+        compiler_params=pltpu.CompilerParams(
+            collective_id=1, has_side_effects=True, vmem_limit_bytes=VMEM_BYTES
+        ),
+    )(d_qkv, d_packed)
 
 
 def shards(blocks, cotangent, modality, time_rank, qkv_weight, out_weight, norm_gain):
-    w_qkv = lax.all_gather(qkv_weight, "dp", axis=1, tiled=True)
-    w_out = lax.all_gather(out_weight, "dp", axis=1, tiled=True)
-    gain = lax.all_gather(norm_gain, "dp", axis=1, tiled=True)
-    encoded, block_grad, d_qkv, d_out, d_gain = encode_own(
-        modality, time_rank, blocks, cotangent, w_qkv, w_out, gain
+    rows, width = out_weight.shape[1:]
+    share = norm_gain.shape[1]
+    start = lax.axis_index("dp") * share
+    padded = -(-(rows + 1) // 8) * 8
+    packed = jnp.concatenate(
+        [
+            out_weight,
+            lax.dynamic_update_slice(
+                jnp.zeros((2, padded - rows, width), jnp.bfloat16), norm_gain[:, None, :], (0, 0, start)
+            ),
+        ],
+        axis=1,
     )
-    kind = lax.axis_index("grp") // 2
-
-    def shared(grad):
-        part = lax.psum_scatter(grad.astype(jnp.float32), "dp", scatter_dimension=1, tiled=True)
-        return lax.dynamic_index_in_dim(lax.psum(part, "grp"), kind, 0, keepdims=True)
-
-    return (encoded, block_grad, shared(d_qkv), shared(d_out), shared(d_gain[:, 0, :]))
+    w_qkv, w_packed = gather_weights(qkv_weight, packed)
+    count = 2 * RING * RING
+    encoded, block_grad, d_qkv, d_packed = encode_own(
+        modality,
+        time_rank,
+        blocks,
+        cotangent,
+        w_qkv.reshape(2, width, -1),
+        w_packed.reshape(2, count, padded, width),
+    )
+    share_qkv, share_packed = scatter_grads(d_qkv.reshape(w_qkv.shape), d_packed.reshape(w_packed.shape))
+    share_gain = lax.dynamic_slice(share_packed, (rows, start), (1, share))
+    return (encoded, block_grad, share_qkv[None], share_packed[None, :rows], share_gain)
 
 
 def solution(mesh):

time: 561 us -> 161 us (0.29)
  waiting for transfers between devices: 310 us -> 0 us
  blocking collectives: 156 us -> 0 us
  Pallas kernels: 45.6 us -> 153 us
  between operations: 15.1 us -> 0.67 us
  local copies, waits for them, and re-layouts: 19.5 us -> 6.42 us
  other arithmetic: 12.2 us -> 0.68 us
    reduce_scatter x1 -> x0, waiting for transfers between devices: 127 us -> none  [shared(): lax.psum_scatter(grad.astype(jnp.float32), 'dp', scatter_dimension=1, til...]
    unnamed x1 -> x0, blocking collectives: 125 us -> none
    pallas_call x0 -> x2, Pallas kernels: none -> 108 us  [the longest x1 60.9 us: scatter_grads(): pl.pallas_call(scatter_kernel, out_shape=(jax.ShapeDtypeStruct(q, f32), j...]
    unnamed x6 -> x0, waiting for transfers between devices: 103 us -> none
    all_gather x2 -> x0, waiting for transfers between devices: 79.9 us -> none  [the longest x1 54 us: shards(): w_qkv = lax.all_gather(qkv_weight, 'dp', axis=1, tiled=True)]
    all_gather x1 -> x0, blocking collectives: 22.9 us -> none  [shards(): gain = lax.all_gather(norm_gain, 'dp', axis=1, tiled=True)]
    convert_element_type x1 -> x0, other arithmetic: 12.2 us -> none  [shared(): grad.astype(jnp.float32)]
    psum x1 -> x0, blocking collectives: 8.56 us -> none  [shared(): lax.psum(part, 'grp')]
  transfers between devices with their start and end apart: 5 -> 0, of which waited for: 4 -> 0; matrix products, arithmetic and copies ran while one was open for 4% -> 0% of each run, Pallas kernels for 0% -> 0%
where the time goes in v2:
time: 161 us; the launch traced here: 160 us
  Pallas kernels  153 us (95%)
  local copies, waits for them, and re-layouts  6.42 us (4%)
    pallas_call x1, Pallas kernels, scatter_grads(): pl.pallas_call(scatter_kernel, out_shape=(jax.ShapeDtypeStruct(q, f32), j...  60.9 us
    pallas_call x1, Pallas kernels, gather_weights(): pl.pallas_call(gather_kernel, out_shape=(jax.ShapeDtypeStruct(shape + qkv...  47.4 us
    pallas_call x1, Pallas kernels, encode_own(): pl.pallas_call(encode_kernel, out_shape=(jax.ShapeDtypeStruct(blocks.shap...  44.4 us
    unnamed x3, local copies, waits for them, and re-layouts  3.36 us

profile of v2, /device:TPU:2, one launch (start us, length us, event | category | flops | bytes accessed | tf_op | source)
XLA Modules:
  0.0 160.4 jit_solution(7987205859078489596)
XLA Ops:
  0.6 0.7 copy.12
  1.3 0.2 dynamic_update_slice.3
  1.5 0.9 copy.13
  2.4 0.7 pad_maximum_fusion.wo_in
  3.1 47.4 %shard_map.110 = (bf16[2,4,4,2,40,1920]{5,4,3,2,1,0:T(8,128)(2,1)}, bf16[2,4,4,2,24,1280]{5,4,3,2,1,0:T(8,128)(2,1)}) custom-call(bf16[2,40,1920]{2,1,0:T(8,128)(2,1)} %wq_in.1, bf16[2,24,1280]{2,1,0:T(8,128)(2,1)} %pad_maximum_fusion.wo_in), custom_call_target="tpu_custom_call" | custom-call | tf_op jit(solution)/shard_map/pallas_call | solution.py:372
  50.5 44.4 %shard_map.111 = (bf16[4,128,1280]{2,1,0:T(8,128)(2,1)}, bf16[4,128,1280]{2,1,0:T(8,128)(2,1)}, bf16[2,1280,1920]{2,1,0:T(8,128)(2,1)}, bf16[2,32,24,1280]{3,2,1,0:T(8,128)(2,1)}) custom-call(s32[4]{0:T(128)} %kind_ref.1, s32[4]{0:T(128)} %rank_ref.1, bf16[4,128,1280]{2,1,0:T(8,128)(2,1)} %x_ref.1, bf16[4,128,1280]{2,1,0:T(8,128)(2,1)} %cot_ref.1, ...), custom_call_target="tpu_custom_call" | custom-call | tf_op jit(solution)/shard_map/pallas_call | solution.py:222
  94.9 60.9 %shard_map.112 = (f32[40,1920]{1,0:T(8,128)}, f32[24,1280]{1,0:T(8,128)}) custom-call(bf16[2,4,4,2,40,1920]{5,4,3,2,1,0:T(8,128)(2,1)} %bitcast.8, bf16[2,4,4,2,24,1280]{5,4,3,2,1,0:T(8,128)(2,1)} %bitcast.10), custom_call_target="tpu_custom_call" | custom-call | tf_op jit(solution)/shard_map/pallas_call | solution.py:553
  155.8 1.3 constant_dynamic-slice_fusion
  157.1 0.9 slice_bitcast_fusion
  158.0 0.7 copy.14
  158.7 1.7 %copy.17 = f32[1,40,1920]{2,1,0:T(8,128)} copy(f32[1,40,1920]{2,1,0:T(8,128)} %bitcast.12) | data formatting | bytes 614400
  (1 shorter events, 0.0 us)

commit v3 on v1

v3 whole, which is shorter than its diff:
```python
import math

import jax
import jax.numpy as jnp
from jax import lax
from jax.experimental import pallas as pl
from jax.experimental.pallas import tpu as pltpu
from jax.sharding import PartitionSpec as P

A_HEADS = 10
A_SIZE = 64
V_HEADS = 8
V_SIZE = 80
WIN = 128
VWIN = 64
LANES = 128
EPSILON = 1e-05
VMEM_BYTES = 62 * 1024 * 1024
RING = 4
CHIPS = RING * RING
STEPS = 35
MESH = pl.DeviceIdType.MESH
OFFSETS = (0, -1, 1, 2)
UP = (True, False, False, True)
BF16, F32 = jnp.bfloat16, jnp.float32


def normalized(x):
    mean_row = jnp.mean(x, axis=-1, keepdims=True)
    centered = x - mean_row
    inverse = lax.rsqrt(jnp.mean(centered * centered, axis=-1, keepdims=True) + EPSILON)
    return centered * inverse, inverse


def nt_dot(a, b):
    return lax.dot_general(a, b, (((1,), (1,)), ((), ())), preferred_element_type=F32)


def tn_dot(a, b):
    return lax.dot_general(a, b, (((0,), (0,)), ((), ())), preferred_element_type=F32)


def nn_dot(a, b):
    return jnp.dot(a, b, preferred_element_type=F32)


def attend_pair(query, keys, values, cot, first, second, scale, same_window):
    zero = jnp.zeros((), BF16)

    def stacked(rows):
        return jnp.concatenate(
            [jnp.where(first, rows, zero), jnp.where(second, rows, zero)], axis=0
        )

    query_two = stacked(query)
    cot_two = stacked(cot)
    scores = jnp.where(same_window, nt_dot(query_two, keys) * scale, -1e30)
    row_max = jnp.max(scores, axis=-1, keepdims=True)
    exponent = jnp.exp(scores - row_max)
    probs = exponent * (1.0 / jnp.sum(exponent, axis=-1, keepdims=True))
    probs_low = probs.astype(BF16)
    d_probs = nt_dot(cot_two, values)
    inner = jnp.sum(d_probs * probs, axis=-1, keepdims=True)
    d_scores = (probs * (d_probs - inner) * scale).astype(BF16)

    def beside(rows):
        return jnp.concatenate([rows[:WIN], rows[WIN:]], axis=1)

    mixed = nn_dot(beside(probs_low), stacked(values))
    d_values = tn_dot(probs_low, cot_two)
    d_query = nn_dot(beside(d_scores), stacked(keys))
    d_keys = tn_dot(d_scores, query_two)
    return mixed, d_query, d_keys, d_values


def attend_block(audio, qkv, cot, out, d_qkv):
    inner = cot.shape[1]
    tile_count = inner // LANES
    scale = jnp.where(audio, 1.0 / math.sqrt(A_SIZE), 1.0 / math.sqrt(V_SIZE)).astype(F32)
    size = jnp.where(audio, A_SIZE, V_SIZE)
    row = lax.broadcasted_iota(jnp.int32, (2 * WIN, WIN), 0)
    col = lax.broadcasted_iota(jnp.int32, (2 * WIN, WIN), 1)
    apart = ((row % WIN) // VWIN != col // VWIN).astype(jnp.int32)
    same_window = apart * jnp.where(audio, 0, 1) == 0
    tiles = [[None] * tile_count for _ in range(4)]
    for pair in range(A_HEADS // 2):
        start, stop = pair * LANES, min((pair + 2) * LANES, inner)
        low = jnp.where(audio, 2 * pair * A_SIZE, 2 * pair * V_SIZE)
        lane = lax.broadcasted_iota(jnp.int32, (WIN, stop - start), 1) + start
        first = (lane >= low) & (lane < low + size)
        second = (lane >= low + size) & (lane < low + 2 * size)
        found = attend_pair(
            qkv[:, start:stop],
            qkv[:, inner + start : inner + stop],
            qkv[:, 2 * inner + start : 2 * inner + stop],
            cot[:, start:stop],
            first,
            second,
            scale,
            same_window,
        )
        for which in range(4):
            for tile in range(start // LANES, stop // LANES):
                at = tile * LANES - start
                part = found[which][:, at : at + LANES]
                held = tiles[which][tile]
                tiles[which][tile] = part if held is None else held + part
        at = slice(start, start + LANES)
        out[:, at] = tiles[0][pair].astype(BF16)
        for which in range(3):
            to = slice(which * inner + start, which * inner + start + LANES)
            d_qkv[:, to] = tiles[which + 1][pair].astype(BF16)


def step_on(position, by):
    return lax.rem(position + by + RING, RING)


class Torus:
    def __init__(self):
        self.row = lax.axis_index("grp")
        self.index = lax.axis_index("dp")
        self.core = self.index % 2
        self.y, self.z = self.index // (2 * RING), self.index // 2 % RING

    def chip(self, first_by, second_by, kind):
        y_by = jnp.where(kind == 0, first_by, second_by)
        z_by = jnp.where(kind == 0, second_by, first_by)
        return step_on(self.y, y_by) * RING + step_on(self.z, z_by)

    def near(self, first_by, second_by):
        return (self.row, self.chip(first_by, second_by, self.core) * 2 + self.core)

    def meet(self):
        self.sibling = (self.row, self.index + 1 - 2 * self.core)
        self.across = (RING - 1 - self.row, self.index)
        self.beside = (self.row + 1 - 2 * (self.row % 2), self.index)
        peers = [self.near(1, 0), self.near(-1, 0), self.near(0, 1), self.near(0, -1)]
        peers += [self.sibling, self.across, self.beside]
        barrier = pltpu.get_barrier_semaphore()
        for peer in peers:
            pl.semaphore_signal(barrier, inc=1, device_id=peer, device_id_type=MESH)
        pl.semaphore_wait(barrier, len(peers))


class Lane:
    def __init__(self, base, send_sem, recv_sem, sibling):
        self.base, self.send_sem, self.recv_sem = base, send_sem, recv_sem
        self.sibling = sibling
        self.sent = []

    def copy(self, number, source, target, device):
        return pltpu.make_async_remote_copy(
            src_ref=source,
            dst_ref=target,
            send_sem=self.send_sem.at[self.base + number],
            recv_sem=self.recv_sem.at[self.base + number],
            device_id=device,
            device_id_type=MESH,
        )

    def send(self, number, source, target, device):
        made = self.copy(number, source, target, device)
        made.start()
        self.sent.append(made)

    def arrive(self, number, target):
        self.copy(number, target, target, self.sibling).wait_recv()

    def finish(self):
        for made in self.sent:
            made.wait_send()
        self.sent = []


class Gather(Lane):
    def __init__(self, base, send_sem, recv_sem, torus, held, cut):
        super().__init__(base, send_sem, recv_sem, torus.sibling)
        self.torus, self.held, self.cut = torus, held, cut

    def slot(self, n, j, kind=None):
        kind = self.torus.core if kind is None else kind
        return self.held.at[kind, self.torus.chip(OFFSETS[n], OFFSETS[j], kind)]

    def half(self, n, upper):
        low = self.cut if upper else 0
        size = self.held.shape[-1] - self.cut if upper else self.cut
        chip = self.torus.chip(OFFSETS[n], 0, self.torus.core)
        return self.held.at[self.torus.core, chip, :, pl.ds(low, size)]

    def pass_on(self, number, view, first_by, second_by):
        self.send(number, view, view, self.torus.near(first_by, second_by))

    def share(self, n, j):
        view = self.slot(n, j)
        self.send(16 + 4 * n + j, view, view, self.sibling)

    def along_second(self, n):
        self.pass_on(4 + 2 * n, self.slot(n, 0), 0, 1)
        self.pass_on(5 + 2 * n, self.slot(n, 0), 0, -1)
        self.share(n, 0)

    def begin(self):
        self.pass_on(0, self.slot(0, 0), 1, 0)
        self.pass_on(1, self.slot(0, 0), -1, 0)
        self.along_second(0)

    def ring_back(self):
        self.arrive(0, self.slot(1, 0))
        self.pass_on(2, self.half(1, False), 1, 0)
        self.along_second(1)

    def ring_ahead(self):
        self.arrive(1, self.slot(2, 0))
        self.pass_on(3, self.half(2, True), -1, 0)
        self.along_second(2)

    def ring_far(self):
        self.arrive(2, self.half(3, False))
        self.arrive(3, self.half(3, True))
        self.along_second(3)

    def second_near(self, n):
        self.arrive(4 + 2 * n, self.slot(n, 1))
        if UP[n]:
            self.pass_on(12 + n, self.slot(n, 1), 0, 1)
        self.share(n, 1)
        self.arrive(5 + 2 * n, self.slot(n, 2))
        if not UP[n]:
            self.pass_on(12 + n, self.slot(n, 2), 0, -1)
        self.share(n, 2)

    def second_far(self, n):
        self.arrive(12 + n, self.slot(n, 3))
        self.share(n, 3)

    def other_kind(self):
        for j in range(4):
            for n in range(4):
                self.arrive(16 + 4 * n + j, self.slot(n, j, 1 - self.torus.core))


class Scatter(Lane):
    def __init__(self, base, send_sem, recv_sem, torus, given, total, held, cut):
        super().__init__(base, send_sem, recv_sem, torus.sibling)
        self.torus, self.given, self.total, self.cut = torus, given, total, cut
        self.one, self.two, self.three, self.four, self.kinds, self.leave, self.row_in = held

    def at(self, n, j):
        return self.torus.chip(OFFSETS[n], OFFSETS[j], self.torus.core)

    def part(self, ref, upper):
        low = self.cut if upper else 0
        size = ref.shape[-1] - self.cut if upper else self.cut
        return ref.at[:, pl.ds(low, size)]

    def add(self, target, *terms):
        value = target[...].astype(F32)
        for term in terms:
            value = value + term[...].astype(F32)
        target[...] = value.astype(BF16)

    def give(self, j):
        for n in range(4):
            chip = self.torus.chip(OFFSETS[n], OFFSETS[j], 1 - self.torus.core)
            self.send(4 * j + n, self.given.at[chip], self.total.at[chip], self.sibling)

    def take(self, j, own):
        for n in range(4):
            chip = self.at(n, j)
            self.arrive(4 * j + n, self.total.at[chip])
            value = own(n, chip) + self.total[chip].astype(F32)
            self.total[chip] = value.astype(BF16)

    def send_far(self):
        for n in range(4):
            device = self.torus.near(0, 1 if UP[n] else -1)
            self.send(16 + n, self.total.at[self.at(n, 3)], self.one.at[n], device)

    def send_near(self, j):
        for n in (3, 1, 2, 0):
            if UP[n] == (j == 2):
                self.arrive(16 + n, self.one.at[n])
                self.add(self.total.at[self.at(n, j)], self.one.at[n])
            number, which = (20 + 2 * n, 0) if j == 2 else (21 + 2 * n, 1)
            device = self.torus.near(0, OFFSETS[j])
            self.send(number, self.total.at[self.at(n, j)], self.two.at[n, which], device)

    def close_second(self, n):
        self.arrive(20 + 2 * n, self.two.at[n, 0])
        self.arrive(21 + 2 * n, self.two.at[n, 1])
        self.add(self.total.at[self.at(n, 0)], self.two.at[n, 0], self.two.at[n, 1])

    def first_far(self):
        self.close_second(3)
        view = self.total.at[self.at(3, 0)]
        self.send(28, self.part(view, False), self.part(self.three, False), self.torus.near(1, 0))
        self.send(29, self.part(view, True), self.part(self.three, True), self.torus.near(-1, 0))
        for n in (2, 1, 0):
            self.close_second(n)

    def first_near(self):
        for n, upper, by in ((2, False, 1), (1, True, -1)):
            view = self.total.at[self.at(n, 0)]
            self.arrive(28 + upper, self.part(self.three, upper))
            self.add(self.part(view, upper), self.part(self.three, upper))
            self.send(30 + upper, view, self.four.at[int(upper)], self.torus.near(by, 0))

    def swap(self, split):
        view = self.total.at[self.at(0, 0)]
        self.arrive(30, self.four.at[0])
        self.arrive(31, self.four.at[1])
        value = view[...].astype(F32) + self.four[0].astype(F32) + self.four[1].astype(F32)
        low, high = split(value)
        core = self.torus.core
        self.kinds[core] = jnp.where(core == 0, low, high).astype(BF16)
        self.leave[...] = jnp.where(core == 0, high, low).astype(BF16)
        self.send(32, self.leave, self.kinds.at[core], self.sibling)

    def cross(self):
        kind = self.torus.row // 2
        self.arrive(32, self.kinds.at[1 - self.torus.core])
        self.send(33, self.kinds.at[1 - kind], self.row_in.at[0], self.torus.across)

    def pair_up(self, out):
        kind = self.torus.row // 2
        self.arrive(33, self.row_in.at[0])
        value = self.kinds[kind].astype(F32) + self.row_in[0].astype(F32)
        out[...] = value
        self.row_in[1] = value.astype(BF16)
        self.send(34, self.row_in.at[1], self.row_in.at[2], self.torus.beside)

    def end(self, out):
        self.arrive(34, self.row_in.at[2])
        out[...] += self.row_in[2].astype(F32)


def layer_kernel(
    kind_ref, rank_ref, x_ref, cot_ref, q_in, o_in, gain_in,
    enc_ref, grad_ref, out_q, out_o,
    wq, wp, wo, gain_s, sib_q, sib_o, sib_gain, xhat_s, inv_s, qkv_s, dattn_s, mixed_s, dqkv_s, ht_s, mt_s,
    y_s, dx_s, dgain_s, give_q, give_o, total_q, total_o, *rest,
):
    held_q, held_o = rest[0:14:2], rest[1:14:2]
    gather_send, gather_recv, scatter_send, scatter_recv = rest[14:]
    blocks, window, width = x_ref.shape
    inner = wo.shape[1]
    rows = inner // CHIPS
    share = width // CHIPS
    padded = wp.shape[2]
    torus = Torus()
    torus.meet()
    core = torus.core
    first = core == 0

    early = Lane(2 * 32, gather_send, gather_recv, torus.sibling)
    early.send(0, o_in.at[1 - core], sib_o, torus.sibling)
    early.send(1, gain_in.at[1 - core], sib_gain, torus.sibling)
    early.send(2, q_in.at[1 - core], sib_q, torus.sibling)
    gather_o = Gather(0, gather_send, gather_recv, torus, wp, width // 2)
    gather_q = Gather(32, gather_send, gather_recv, torus, wq, 1024)
    gathers = (gather_o, gather_q)
    here = torus.y * RING + torus.z
    early.arrive(0, sib_o)
    early.arrive(1, sib_gain)
    mine, other = o_in[core].astype(F32), sib_o[...].astype(F32)
    gain_row = gain_in[core] + sib_gain[...]
    wp[core, here] = jnp.concatenate(
        [
            jnp.where(first, mine, other),
            jnp.where(first, other, mine),
            gain_row,
            jnp.zeros((padded - 2 * mine.shape[0] - 1, width), F32),
        ],
        axis=0,
    ).astype(BF16)
    gather_o.begin()
    early.arrive(2, sib_q)
    mine, other = q_in[core].astype(F32), sib_q[...].astype(F32)
    wq[core, here] = jnp.concatenate(
        [jnp.where(first, mine, other), jnp.where(first, other, mine)], axis=0
    ).astype(BF16)
    gather_q.begin()

    def norm_block(b):
        x_hat, inverse = normalized(x_ref[b].astype(F32))
        xhat_s[b] = x_hat
        inv_s[b] = jnp.broadcast_to(inverse, inv_s.shape[1:])

    norm_block(0)
    for one in gathers:
        one.ring_back()
        one.ring_ahead()
    norm_block(1)
    for one in gathers:
        one.second_near(0)
    norm_block(2)
    for one in gathers:
        one.ring_far()
    norm_block(3)
    for one in gathers:
        one.second_near(1)
        one.second_near(2)
        one.second_far(0)
    for one in gathers:
        one.second_near(3)
        one.second_far(1)
        one.second_far(2)
        one.second_far(3)
    gather_o.other_kind()

    @pl.loop(0, 2)
    def _(m):
        for chip in range(0, CHIPS, 2):
            two = [wp[m, chip + i, 0:rows].astype(F32) for i in range(2)]
            wo[m, chip * rows : (chip + 2) * rows] = jnp.concatenate(two, axis=0).astype(BF16)
        gain_s[m] = sum(wp[m, chip, rows : rows + 1].astype(F32) for chip in range(CHIPS))

    gather_q.other_kind()

    def weights(kind, low, high):
        return wq[kind, :, :, low:high].reshape(width, high - low)

    @pl.loop(0, blocks)
    def _(b):
        kind = kind_ref[b]
        normed = (xhat_s[b] * gain_s[kind]).astype(BF16)
        columns = pl.ds(pl.multiple_of(b * WIN, WIN), WIN)
        turned = normed.T
        for m in range(2):
            ht_s[m, :, columns] = jnp.where(kind == m, turned, jnp.zeros_like(turned))
        for at in range(0, 3 * inner, inner):
            qkv_s[:, at : at + inner] = nn_dot(normed, weights(kind, at, at + inner)).astype(BF16)
        dattn_s[...] = nt_dot(cot_ref[b], wo[kind]).astype(BF16)
        attend_block(kind == 0, qkv_s, dattn_s, mixed_s.at[b], dqkv_s.at[b])
        mixed_t = mixed_s[b].T
        for m in range(2):
            mt_s[m, :, columns] = jnp.where(kind == m, mixed_t, jnp.zeros_like(mixed_t))

    scatter_q = Scatter(
        0, scatter_send, scatter_recv, torus, give_q, total_q, held_q, 1024
    )
    scatter_o = Scatter(
        STEPS, scatter_send, scatter_recv, torus, give_o, total_o, held_o, width // 2
    )
    tokens = blocks * window
    d_qkv_all = dqkv_s[...].reshape(tokens, 3 * inner)

    def q_block(kind, j):
        parts = []
        for n in range(4):
            chip = torus.chip(OFFSETS[n], OFFSETS[j], kind)
            at = pl.ds(pl.multiple_of(chip * share, 16), share)
            parts.append(ht_s[kind, at, :])
        return nn_dot(jnp.concatenate(parts, axis=0), d_qkv_all)

    for j in (3, 2, 1, 0):
        found = q_block(1 - core, j)
        for n in range(4):
            chip = torus.chip(OFFSETS[n], OFFSETS[j], 1 - core)
            give_q[chip] = found[n * share : (n + 1) * share].astype(BF16)
        scatter_q.give(j)

    def take_q(j):
        found = q_block(core, j)
        scatter_q.take(j, lambda n, chip: found[n * share : (n + 1) * share])

    take_q(3)
    scatter_q.send_far()
    take_q(2)
    scatter_q.send_near(2)
    take_q(1)
    scatter_q.send_near(1)
    take_q(0)
    dgain_s[...] = jnp.zeros_like(dgain_s)

    def finish_blocks(low, high):
        @pl.loop(low, high)
        def _(b):
            kind = kind_ref[b]
            x_hat = xhat_s[b]
            gain = gain_s[kind]
            y = x_ref[b].astype(F32) + nn_dot(mixed_s[b], wo[kind])
            y_s[b] = y.astype(BF16)
            d_normed = nt_dot(dqkv_s[b], weights(kind, 0, 3 * inner))
            d_gain = jnp.sum(d_normed * x_hat, axis=0, keepdims=True)
            for m in range(2):
                dgain_s[m] += jnp.where(kind == m, d_gain, jnp.zeros_like(d_gain))
            scaled = d_normed * gain
            d_input = inv_s[b][:, 0:1] * (
                scaled
                - jnp.mean(scaled, axis=-1, keepdims=True)
                - x_hat * jnp.mean(scaled * x_hat, axis=-1, keepdims=True)
            )
            dx_s[b] = (cot_ref[b].astype(F32) + d_input).astype(BF16)

    finish_blocks(0, blocks)
    cot_all = cot_ref[...].reshape(tokens, width)

    def o_rows(kind, store):
        below = jnp.concatenate(
            [dgain_s[kind], jnp.zeros((padded - rows - 1, width), F32)], axis=0
        )
        for at in range(0, CHIPS, 4):
            four = nn_dot(mt_s[kind, at * rows : (at + 4) * rows, :], cot_all)
            for i in range(4):
                store(at + i, jnp.concatenate([four[i * rows : (i + 1) * rows], below], axis=0))

    def store_given(chip, value):
        give_o[chip] = value.astype(BF16)

    o_rows(1 - core, store_given)
    for j in (3, 2, 1, 0):
        scatter_o.give(j)
    scatter_q.first_far()
    gather_o.finish()

    def keep_own(chip, value):
        wp[core, chip] = value.astype(BF16)

    o_rows(core, keep_own)
    scatter_q.first_near()

    def take_o(j):
        scatter_o.take(j, lambda n, chip: wp[core, chip].astype(F32))

    take_o(3)
    scatter_o.send_far()
    scatter_q.swap(lambda value: (value[:share // 2], value[share // 2 :]))
    take_o(2)
    take_o(1)
    scatter_o.send_near(2)
    scatter_o.send_near(1)
    take_o(0)
    scatter_q.cross()
    for r in range(blocks):
        y, dx = y_s[0], dx_s[0]
        for b in range(1, blocks):
            y = jnp.where(rank_ref[b] == r, y_s[b], y)
            dx = jnp.where(rank_ref[b] == r, dx_s[b], dx)
        enc_ref[r] = y
        grad_ref[r] = dx
    scatter_o.first_far()
    scatter_q.pair_up(out_q)
    scatter_o.first_near()

    def split_o(value):
        half = rows // 2
        below = jnp.concatenate([value[rows : rows + 1], jnp.zeros((3, width), F32)], axis=0)
        return (
            jnp.concatenate([value[:half], below], axis=0),
            jnp.concatenate([value[half:rows], below], axis=0),
        )

    scatter_o.swap(split_o)
    scatter_q.end(out_q)
    scatter_o.cross()
    scatter_o.pair_up(out_o)
    scatter_o.end(out_o)
    for one in (early, gather_o, gather_q, scatter_q, scatter_o):
        one.finish()


def layer(kind, rank, blocks, cotangent, qkv_weight, out_weight, gain_row):
    count, window, width = blocks.shape
    inner = qkv_weight.shape[2] // 3
    tokens = count * window
    rows = inner // CHIPS
    padded = -(-(rows + 1) // 16) * 16
    q, o = (width // CHIPS, 3 * inner), (padded, width)
    half_q, half_o = qkv_weight.shape[1:], (-(-(rows // 2 + 1) // 8) * 8, width)
    scratch = [
        pltpu.VMEM((2, CHIPS) + q, BF16),
        pltpu.VMEM((2, CHIPS) + o, BF16),
        pltpu.VMEM((2, inner, width), BF16),
        pltpu.VMEM((2, 1, width), F32),
        pltpu.VMEM(qkv_weight.shape[1:], BF16),
        pltpu.VMEM(out_weight.shape[1:], BF16),
        pltpu.VMEM((1, width), F32),
        pltpu.VMEM((count, window, width), F32),
        pltpu.VMEM((count, window, LANES), F32),
        pltpu.VMEM((window, 3 * inner), BF16),
        pltpu.VMEM((window, inner), BF16),
        pltpu.VMEM((count, window, inner), BF16),
        pltpu.VMEM((count, window, 3 * inner), BF16),
        pltpu.VMEM((2, width, tokens), BF16),
        pltpu.VMEM((2, inner, tokens), BF16),
        pltpu.VMEM((count, window, width), BF16),
        pltpu.VMEM((count, window, width), BF16),
        pltpu.VMEM((2, 1, width), F32),
        pltpu.VMEM((CHIPS,) + q, BF16),
        pltpu.VMEM((CHIPS,) + o, BF16),
        pltpu.VMEM((CHIPS,) + q, BF16),
        pltpu.VMEM((CHIPS,) + o, BF16),
    ]
    for lead in ((4,), (4, 2), (), (2,)):
        scratch += [pltpu.VMEM(lead + q, BF16), pltpu.VMEM(lead + o, BF16)]
    for lead in ((2,), (), (3,)):
        scratch += [pltpu.VMEM(lead + half_q, BF16), pltpu.VMEM(lead + half_o, BF16)]
    scratch += [pltpu.SemaphoreType.DMA((2 * 32 + 3,))] * 2
    scratch += [pltpu.SemaphoreType.DMA((2 * STEPS,))] * 2
    vmem = pl.BlockSpec(memory_space=pltpu.VMEM)
    return pl.pallas_call(
        layer_kernel,
        out_shape=(
            jax.ShapeDtypeStruct(blocks.shape, BF16),
            jax.ShapeDtypeStruct(blocks.shape, BF16),
            jax.ShapeDtypeStruct(half_q, F32),
            jax.ShapeDtypeStruct(half_o, F32),
        ),
        in_specs=[pl.BlockSpec(memory_space=pltpu.SMEM)] * 2 + [vmem] * 5,
        out_specs=(vmem,) * 4,
        scratch_shapes=scratch,
        compiler_params=pltpu.CompilerParams(
            collective_id=0, has_side_effects=True, vmem_limit_bytes=VMEM_BYTES
        ),
    )(kind, rank, blocks, cotangent, qkv_weight, out_weight, gain_row)


def shards(blocks, cotangent, modality, time_rank, qkv_weight, out_weight, norm_gain):
    rows, width = out_weight.shape[1:]
    share = norm_gain.shape[1]
    start = lax.axis_index("dp") * share
    gain_row = lax.dynamic_update_slice(
        jnp.zeros((2, width), F32), norm_gain.astype(F32), (0, start)
    )[:, None, :]
    encoded, block_grad, share_qkv, share_packed = layer(
        modality, time_rank, blocks, cotangent, qkv_weight, out_weight, gain_row
    )
    share_gain = lax.dynamic_slice(share_packed, (rows, start), (1, share))
    return (encoded, block_grad, share_qkv[None], share_packed[None, :rows], share_gain)


def solution(mesh):
    return jax.shard_map(
        shards,
        mesh=mesh,
        in_specs=(
            P(("grp", "dp"), None, None),
            P(("grp", "dp"), None, None),
            P(("grp", "dp")),
            P(("grp", "dp")),
            P(None, "dp", None),
            P(None, "dp", None),
            P(None, "dp"),
        ),
        out_specs=(
            P(("grp", "dp"), None, None),
            P(("grp", "dp"), None, None),
            P("grp", "dp", None),
            P("grp", "dp", None),
            P("grp", "dp"),
        ),
        check_vma=False,
    )
```

time: 561 us -> 142 us (0.25)
  waiting for transfers between devices: 310 us -> 0 us
  blocking collectives: 156 us -> 0 us
  Pallas kernels: 45.6 us -> 131 us
  between operations: 15.1 us -> 0.67 us
  other arithmetic: 12.2 us -> 0.66 us
  local copies, waits for them, and re-layouts: 19.5 us -> 9.12 us
    reduce_scatter x1 -> x0, waiting for transfers between devices: 127 us -> none  [shared(): lax.psum_scatter(grad.astype(jnp.float32), 'dp', scatter_dimension=1, til...]
    unnamed x1 -> x0, blocking collectives: 125 us -> none
    unnamed x6 -> x0, waiting for transfers between devices: 103 us -> none
    pallas_call x1, Pallas kernels: 45.6 us -> 131 us  [layer(): pl.pallas_call(layer_kernel, out_shape=(jax.ShapeDtypeStruct(blocks.shape...]
    all_gather x2 -> x0, waiting for transfers between devices: 79.9 us -> none  [the longest x1 54 us: shards(): w_qkv = lax.all_gather(qkv_weight, 'dp', axis=1, tiled=True)]
    all_gather x1 -> x0, blocking collectives: 22.9 us -> none  [shards(): gain = lax.all_gather(norm_gain, 'dp', axis=1, tiled=True)]
    convert_element_type x1 -> x0, other arithmetic: 12.2 us -> none  [shared(): grad.astype(jnp.float32)]
    psum x1 -> x0, blocking collectives: 8.56 us -> none  [shared(): lax.psum(part, 'grp')]
  transfers between devices with their start and end apart: 5 -> 0, of which waited for: 4 -> 0; matrix products, arithmetic and copies ran while one was open for 4% -> 0% of each run, Pallas kernels for 0% -> 0%
where the time goes in v3:
time: 142 us
  Pallas kernels  131 us (92%)
  local copies, waits for them, and re-layouts  9.12 us (6%)
    pallas_call x1, Pallas kernels, layer(): pl.pallas_call(layer_kernel, out_shape=(jax.ShapeDtypeStruct(blocks.shape...  131 us
    unnamed x11, local copies, waits for them, and re-layouts  6.75 us

profile of v3, /device:TPU:2, one launch (start us, length us, event | category | flops | bytes accessed | tf_op | source)
XLA Modules:
  0.0 141.9 jit_solution(11643148136741937678)
XLA Ops:
  0.6 0.7 bitcast_convert_fusion
  1.3 0.2 dynamic_update_slice.4.gain_in
  1.5 0.0 copy-start.2
  1.5 1.6 %copy.13.o_in = bf16[2,20,1280]{2,1,0:T(8,128)(2,1)} copy(bf16[2,20,1280]{2,0,1:T(2,128)(2,1)} %param.12) | data formatting | bytes 204800 | tf_op args[5]
  3.0 0.0 copy-done.2
  3.1 131.5 %shard_map.110 = (bf16[4,128,1280]{2,1,0:T(8,128)(2,1)}, bf16[4,128,1280]{2,1,0:T(8,128)(2,1)}, f32[40,1920]{1,0:T(8,128)}, f32[24,1280]{1,0:T(8,128)}) custom-call(s32[4]{0:T(128)} %kind_ref.1, s32[4]{0:T(128)} %rank_ref.1, bf16[4,128,1280]{2,1,0:T(8,128)(2,1)} %x_ref.1, bf16[4,128,1280]{2,1,0:T(8,128)(2,1)} %cot_ref.1, bf16[2,40,1920]{2,1,0:T(8,128)(2,1)} %q_in.1, ...), custom_call_target="tpu_custom_call" | custom-call | tf_op jit(solution)/shard_map/pallas_call | solution.py:603
  134.5 1.3 constant_dynamic-slice_fusion
  135.8 0.9 slice_bitcast_fusion
  136.7 0.7 copy.14
  137.5 0.0 copy-start
  137.5 2.6 %copy.19 = bf16[4,128,1280]{2,1,0:T(8,128)(2,1)} copy(bf16[4,128,1280]{2,1,0:T(8,128)(2,1)} %get-tuple-element.23) | data formatting | bytes 2621440
  140.0 0.0 copy-done
  140.0 0.0 copy-start.1
  140.0 1.1 copy.20
  141.1 0.1 copy-done.1
  141.2 0.7 copy.21
  (1 shorter events, 0.0 us)
Async XLA Ops:
  1.5 1.6 %copy-start.2 = (f32[2,1,1280]{2,1,0:T(1,128)}, f32[2,1,1280]{2,1,0:T(1,128)S(1)}, u32[]{:S(2)}) copy-start(f32[2,1,1280]{2,1,0:T(1,128)S(1)} %dynamic_update_slice.4.gain_in) | copy-start | bytes 30724
  137.5 2.6 %copy-start = (bf16[4,128,1280]{2,1,0:T(8,128)(2,1)S(1)}, bf16[4,128,1280]{2,1,0:T(8,128)(2,1)}, u32[]{:S(2)}) copy-start(bf16[4,128,1280]{2,1,0:T(8,128)(2,1)} %get-tuple-element.24) | copy-start | bytes 3932164
  140.0 1.2 copy-start.1

commit v4 on v3

--- a/solution.py
+++ b/solution.py
@@ -15,10 +15,12 @@
 VWIN = 64
 LANES = 128
 EPSILON = 1e-05
-VMEM_BYTES = 62 * 1024 * 1024
+VMEM_BYTES = 63 * 1024 * 1024
 RING = 4
 CHIPS = RING * RING
-STEPS = 35
+STEPS = 51
+BEHIND = 6
+AWAY_Q, AWAY_O = 5 * LANES, 3 * LANES
 MESH = pl.DeviceIdType.MESH
 OFFSETS = (0, -1, 1, 2)
 UP = (True, False, False, True)
@@ -173,86 +175,125 @@
         self.sent = []
 
 
-class Gather(Lane):
-    def __init__(self, base, send_sem, recv_sem, torus, held, cut):
+class Slots(Lane):
+    def __init__(self, base, send_sem, recv_sem, torus, columns, away):
         super().__init__(base, send_sem, recv_sem, torus.sibling)
-        self.torus, self.held, self.cut = torus, held, cut
-
-    def slot(self, n, j, kind=None):
-        kind = self.torus.core if kind is None else kind
-        return self.held.at[kind, self.torus.chip(OFFSETS[n], OFFSETS[j], kind)]
+        self.torus, self.away, self.carried = torus, away, columns - away
+        odd = torus.row % 2
+        self.start = pl.multiple_of(away * (1 - odd), LANES)
+        self.missing = pl.ds(pl.multiple_of(self.carried * odd, LANES), away)
+        self.lent = pl.ds(pl.multiple_of(self.carried * (1 - odd), LANES), away)
+        self.cut = -(-self.carried // (2 * LANES)) * LANES
+
+    def chip(self, n, j):
+        return self.torus.chip(OFFSETS[n], OFFSETS[j], self.torus.core)
+
+    def window(self):
+        return pl.ds(self.start, self.carried)
+
+    def half_window(self, upper):
+        if upper:
+            return pl.ds(self.start + self.cut, self.carried - self.cut)
+        return pl.ds(self.start, self.cut)
+
+    def neighbour(self, n, j):
+        return self.torus.across if (n + j) % 2 else self.torus.beside
+
+
+class Gather(Slots):
+    def __init__(self, base, send_sem, recv_sem, torus, held, away, pending):
+        super().__init__(base, send_sem, recv_sem, torus, held.shape[-1], away)
+        self.held, self.pending = held, pending
+
+    def slot(self, n, j, columns=None):
+        columns = self.window() if columns is None else columns
+        return self.held.at[self.torus.core, self.chip(n, j), :, columns]
 
     def half(self, n, upper):
-        low = self.cut if upper else 0
-        size = self.held.shape[-1] - self.cut if upper else self.cut
-        chip = self.torus.chip(OFFSETS[n], 0, self.torus.core)
-        return self.held.at[self.torus.core, chip, :, pl.ds(low, size)]
+        return self.slot(n, 0, self.half_window(upper))
 
     def pass_on(self, number, view, first_by, second_by):
         self.send(number, view, view, self.torus.near(first_by, second_by))
 
     def share(self, n, j):
-        view = self.slot(n, j)
+        view = self.held.at[self.torus.core, self.chip(n, j)]
         self.send(16 + 4 * n + j, view, view, self.sibling)
+
+    def lend(self, n, j):
+        view = self.slot(n, j, self.lent)
+        self.send(32 + 4 * n + j, view, view, self.neighbour(n, j))
+        self.pending.append((self, n, j))
+        if len(self.pending) > BEHIND:
+            one, n, j = self.pending.pop(0)
+            one.complete(n, j)
+
+    def complete(self, n, j):
+        self.arrive(32 + 4 * n + j, self.slot(n, j, self.missing))
+        self.share(n, j)
 
     def along_second(self, n):
         self.pass_on(4 + 2 * n, self.slot(n, 0), 0, 1)
         self.pass_on(5 + 2 * n, self.slot(n, 0), 0, -1)
-        self.share(n, 0)
 
     def begin(self):
         self.pass_on(0, self.slot(0, 0), 1, 0)
         self.pass_on(1, self.slot(0, 0), -1, 0)
         self.along_second(0)
+        self.share(0, 0)
 
     def ring_back(self):
         self.arrive(0, self.slot(1, 0))
         self.pass_on(2, self.half(1, False), 1, 0)
         self.along_second(1)
+        self.lend(1, 0)
 
     def ring_ahead(self):
         self.arrive(1, self.slot(2, 0))
         self.pass_on(3, self.half(2, True), -1, 0)
         self.along_second(2)
+        self.lend(2, 0)
 
     def ring_far(self):
         self.arrive(2, self.half(3, False))
         self.arrive(3, self.half(3, True))
         self.along_second(3)
+        self.lend(3, 0)
 
     def second_near(self, n):
         self.arrive(4 + 2 * n, self.slot(n, 1))
         if UP[n]:
             self.pass_on(12 + n, self.slot(n, 1), 0, 1)
-        self.share(n, 1)
+        self.lend(n, 1)
         self.arrive(5 + 2 * n, self.slot(n, 2))
         if not UP[n]:
             self.pass_on(12 + n, self.slot(n, 2), 0, -1)
-        self.share(n, 2)
+        self.lend(n, 2)
 
     def second_far(self, n):
         self.arrive(12 + n, self.slot(n, 3))
-        self.share(n, 3)
+        self.lend(n, 3)
 
     def other_kind(self):
+        other = 1 - self.torus.core
         for j in range(4):
             for n in range(4):
-                self.arrive(16 + 4 * n + j, self.slot(n, j, 1 - self.torus.core))
-
-
-class Scatter(Lane):
-    def __init__(self, base, send_sem, recv_sem, torus, given, total, held, cut):
-        super().__init__(base, send_sem, recv_sem, torus.sibling)
-        self.torus, self.given, self.total, self.cut = torus, given, total, cut
-        self.one, self.two, self.three, self.four, self.kinds, self.leave, self.row_in = held
-
-    def at(self, n, j):
-        return self.torus.chip(OFFSETS[n], OFFSETS[j], self.torus.core)
-
-    def part(self, ref, upper):
-        low = self.cut if upper else 0
-        size = ref.shape[-1] - self.cut if upper else self.cut
-        return ref.at[:, pl.ds(low, size)]
+                chip = self.torus.chip(OFFSETS[n], OFFSETS[j], other)
+                self.arrive(16 + 4 * n + j, self.held.at[other, chip])
+
+
+class Scatter(Slots):
+    def __init__(self, base, send_sem, recv_sem, torus, given, total, held, away):
+        super().__init__(base, send_sem, recv_sem, torus, total.shape[-1], away)
+        self.given, self.total = given, total
+        self.one, self.two, self.three, self.four, self.lent_in = held[:5]
+        self.kinds, self.leave, self.row_in = held[5:]
+
+    def view(self, n, j, columns=None):
+        columns = self.window() if columns is None else columns
+        return self.total.at[self.chip(n, j), :, columns]
+
+    def part(self, upper):
+        return self.three.at[:, slice(self.cut, None) if upper else slice(0, self.cut)]
 
     def add(self, target, *terms):
         value = target[...].astype(F32)
@@ -267,82 +308,127 @@
 
     def take(self, j, own):
         for n in range(4):
-            chip = self.at(n, j)
+            chip = self.chip(n, j)
             self.arrive(4 * j + n, self.total.at[chip])
             value = own(n, chip) + self.total[chip].astype(F32)
             self.total[chip] = value.astype(BF16)
+            if n or j:
+                lent = self.view(n, j, self.missing)
+                self.send(32 + 4 * j + n, lent, self.lent_in.at[4 * j + n], self.neighbour(n, j))
+
+    def take_lent(self, j):
+        for n in range(4):
+            if n or j:
+                self.arrive(32 + 4 * j + n, self.lent_in.at[4 * j + n])
+                self.add(self.view(n, j, self.lent), self.lent_in.at[4 * j + n])
 
     def send_far(self):
         for n in range(4):
             device = self.torus.near(0, 1 if UP[n] else -1)
-            self.send(16 + n, self.total.at[self.at(n, 3)], self.one.at[n], device)
+            self.send(16 + n, self.view(n, 3), self.one.at[n], device)
 
     def send_near(self, j):
         for n in (3, 1, 2, 0):
             if UP[n] == (j == 2):
                 self.arrive(16 + n, self.one.at[n])
-                self.add(self.total.at[self.at(n, j)], self.one.at[n])
+                self.add(self.view(n, j), self.one.at[n])
             number, which = (20 + 2 * n, 0) if j == 2 else (21 + 2 * n, 1)
             device = self.torus.near(0, OFFSETS[j])
-            self.send(number, self.total.at[self.at(n, j)], self.two.at[n, which], device)
+            self.send(number, self.view(n, j), self.two.at[n, which], device)
 
     def close_second(self, n):
         self.arrive(20 + 2 * n, self.two.at[n, 0])
         self.arrive(21 + 2 * n, self.two.at[n, 1])
-        self.add(self.total.at[self.at(n, 0)], self.two.at[n, 0], self.two.at[n, 1])
+        self.add(self.view(n, 0), self.two.at[n, 0], self.two.at[n, 1])
 
     def first_far(self):
         self.close_second(3)
-        view = self.total.at[self.at(3, 0)]
-        self.send(28, self.part(view, False), self.part(self.three, False), self.torus.near(1, 0))
-        self.send(29, self.part(view, True), self.part(self.three, True), self.torus.near(-1, 0))
+        for upper, by in ((False, 1), (True, -1)):
+            view = self.view(3, 0, self.half_window(upper))
+            self.send(28 + upper, view, self.part(upper), self.torus.near(by, 0))
         for n in (2, 1, 0):
             self.close_second(n)
 
     def first_near(self):
         for n, upper, by in ((2, False, 1), (1, True, -1)):
-            view = self.total.at[self.at(n, 0)]
-            self.arrive(28 + upper, self.part(self.three, upper))
-            self.add(self.part(view, upper), self.part(self.three, upper))
-            self.send(30 + upper, view, self.four.at[int(upper)], self.torus.near(by, 0))
+            self.arrive(28 + upper, self.part(upper))
+            self.add(self.view(n, 0, self.half_window(upper)), self.part(upper))
+            self.send(30 + upper, self.view(n, 0), self.four.at[int(upper)], self.torus.near(by, 0))
 
     def swap(self, split):
-        view = self.total.at[self.at(0, 0)]
         self.arrive(30, self.four.at[0])
         self.arrive(31, self.four.at[1])
-        value = view[...].astype(F32) + self.four[0].astype(F32) + self.four[1].astype(F32)
-        low, high = split(value)
+        self.add(self.view(0, 0), self.four.at[0], self.four.at[1])
+        low, high = split(self.total[self.chip(0, 0)].astype(F32))
         core = self.torus.core
         self.kinds[core] = jnp.where(core == 0, low, high).astype(BF16)
         self.leave[...] = jnp.where(core == 0, high, low).astype(BF16)
-        self.send(32, self.leave, self.kinds.at[core], self.sibling)
+        self.send(48, self.leave, self.kinds.at[core], self.sibling)
 
     def cross(self):
         kind = self.torus.row // 2
-        self.arrive(32, self.kinds.at[1 - self.torus.core])
-        self.send(33, self.kinds.at[1 - kind], self.row_in.at[0], self.torus.across)
+        self.arrive(48, self.kinds.at[1 - self.torus.core])
+        self.send(49, self.kinds.at[1 - kind], self.row_in.at[0], self.torus.across)
 
     def pair_up(self, out):
         kind = self.torus.row // 2
-        self.arrive(33, self.row_in.at[0])
+        self.arrive(49, self.row_in.at[0])
         value = self.kinds[kind].astype(F32) + self.row_in[0].astype(F32)
         out[...] = value
         self.row_in[1] = value.astype(BF16)
-        self.send(34, self.row_in.at[1], self.row_in.at[2], self.torus.beside)
+        self.send(50, self.row_in.at[1], self.row_in.at[2], self.torus.beside)
 
     def end(self, out):
-        self.arrive(34, self.row_in.at[2])
+        self.arrive(50, self.row_in.at[2])
         out[...] += self.row_in[2].astype(F32)
+
+
+class Exchange(Lane):
+    def __init__(self, base, send_sem, recv_sem, torus, sums, incoming):
+        super().__init__(base, send_sem, recv_sem, torus.sibling)
+        self.torus, self.sums, self.incoming = torus, sums, incoming
+        turn_y, turn_z = 1 - 2 * (torus.y % 2), 1 - 2 * (torus.z % 2)
+        first = jnp.where(torus.core == 0, turn_y, turn_z)
+        second = jnp.where(torus.core == 0, turn_z, turn_y)
+        self.partners = [torus.near(first, 0), torus.near(-first, 0)]
+        self.partners += [torus.near(0, second), torus.near(0, -second), torus.beside, torus.across]
+        self.done = 0
+
+    def begin(self, parts):
+        core = self.torus.core
+        self.send(6, parts.at[1 - core], self.incoming.at[6], self.sibling)
+        self.arrive(6, self.incoming.at[6])
+        self.sums[0] = parts[core] + self.incoming[6]
+        self.start()
+
+    def start(self):
+        k = self.done
+        self.send(k, self.sums.at[k], self.incoming.at[k], self.partners[k])
+
+    def step(self):
+        k = self.done
+        self.arrive(k, self.incoming.at[k])
+        self.sums[k + 1] = self.sums[k] + self.incoming[k]
+        self.done += 1
+        if self.done < 6:
+            self.start()
+        else:
+            self.send(7, self.sums.at[6], self.incoming.at[7], self.sibling)
+
+    def end(self, out):
+        self.arrive(7, self.incoming.at[7])
+        own = self.torus.row // 2 == self.torus.core
+        out[...] = jnp.where(own, self.sums[6], self.incoming[7])
 
 
 def layer_kernel(
     kind_ref, rank_ref, x_ref, cot_ref, q_in, o_in, gain_in,
-    enc_ref, grad_ref, out_q, out_o,
+    enc_ref, grad_ref, out_q, out_o, out_gain,
     wq, wp, wo, gain_s, sib_q, sib_o, sib_gain, xhat_s, inv_s, qkv_s, dattn_s, mixed_s, dqkv_s, ht_s, mt_s,
-    y_s, dx_s, dgain_s, give_q, give_o, total_q, total_o, *rest,
+    dx_s, dgain_s, gain_sums, gain_rows, give_q, give_o, total_q, total_o, *rest,
 ):
-    held_q, held_o = rest[0:14:2], rest[1:14:2]
-    gather_send, gather_recv, scatter_send, scatter_recv = rest[14:]
+    held_q, held_o = rest[0:16:2], rest[1:16:2]
+    gather_send, gather_recv, scatter_send, scatter_recv, gain_send, gain_recv = rest[16:]
     blocks, window, width = x_ref.shape
     inner = wo.shape[1]
     rows = inner // CHIPS
@@ -353,12 +439,13 @@
     core = torus.core
     first = core == 0
 
-    early = Lane(2 * 32, gather_send, gather_recv, torus.sibling)
+    early = Lane(2 * 48, gather_send, gather_recv, torus.sibling)
     early.send(0, o_in.at[1 - core], sib_o, torus.sibling)
     early.send(1, gain_in.at[1 - core], sib_gain, torus.sibling)
     early.send(2, q_in.at[1 - core], sib_q, torus.sibling)
-    gather_o = Gather(0, gather_send, gather_recv, torus, wp, width // 2)
-    gather_q = Gather(32, gather_send, gather_recv, torus, wq, 1024)
+    pending = []
+    gather_o = Gather(0, gather_send, gather_recv, torus, wp, AWAY_O, pending)
+    gather_q = Gather(48, gather_send, gather_recv, torus, wq, AWAY_Q, pending)
     gathers = (gather_o, gather_q)
     here = torus.y * RING + torus.z
     early.arrive(0, sib_o)
@@ -392,21 +479,28 @@
         one.ring_back()
         one.ring_ahead()
     norm_block(1)
-    for one in gathers:
-        one.second_near(0)
+    gather_o.second_near(0)
+    gather_o.ring_far()
+    gather_q.second_near(0)
     norm_block(2)
-    for one in gathers:
-        one.ring_far()
+    gather_o.second_near(1)
+    gather_o.second_near(2)
+    gather_o.second_far(0)
+    gather_q.ring_far()
     norm_block(3)
-    for one in gathers:
-        one.second_near(1)
-        one.second_near(2)
-        one.second_far(0)
-    for one in gathers:
-        one.second_near(3)
-        one.second_far(1)
-        one.second_far(2)
-        one.second_far(3)
+    gather_o.second_near(3)
+    gather_o.second_far(1)
+    gather_o.second_far(2)
+    gather_q.second_near(1)
+    gather_q.second_near(2)
+    gather_q.second_far(0)
+    gather_o.second_far(3)
+    gather_q.second_near(3)
+    gather_q.second_far(1)
+    gather_q.second_far(2)
+    gather_q.second_far(3)
+    for one, n, j in pending:
+        one.complete(n, j)
     gather_o.other_kind()
 
     @pl.loop(0, 2)
@@ -416,32 +510,37 @@
             wo[m, chip * rows : (chip + 2) * rows] = jnp.concatenate(two, axis=0).astype(BF16)
         gain_s[m] = sum(wp[m, chip, rows : rows + 1].astype(F32) for chip in range(CHIPS))
 
-    gather_q.other_kind()
-
     def weights(kind, low, high):
         return wq[kind, :, :, low:high].reshape(width, high - low)
 
     @pl.loop(0, blocks)
     def _(b):
         kind = kind_ref[b]
-        normed = (xhat_s[b] * gain_s[kind]).astype(BF16)
         columns = pl.ds(pl.multiple_of(b * WIN, WIN), WIN)
-        turned = normed.T
+        turned = (xhat_s[b] * gain_s[kind]).astype(BF16).T
         for m in range(2):
             ht_s[m, :, columns] = jnp.where(kind == m, turned, jnp.zeros_like(turned))
+        dattn_s[b] = nt_dot(cot_ref[b], wo[kind]).astype(BF16)
+
+    gather_q.other_kind()
+
+    @pl.loop(0, blocks)
+    def _(b):
+        kind = kind_ref[b]
+        columns = pl.ds(pl.multiple_of(b * WIN, WIN), WIN)
+        normed = (xhat_s[b] * gain_s[kind]).astype(BF16)
         for at in range(0, 3 * inner, inner):
             qkv_s[:, at : at + inner] = nn_dot(normed, weights(kind, at, at + inner)).astype(BF16)
-        dattn_s[...] = nt_dot(cot_ref[b], wo[kind]).astype(BF16)
-        attend_block(kind == 0, qkv_s, dattn_s, mixed_s.at[b], dqkv_s.at[b])
+        attend_block(kind == 0, qkv_s, dattn_s.at[b], mixed_s.at[b], dqkv_s.at[b])
         mixed_t = mixed_s[b].T
         for m in range(2):
             mt_s[m, :, columns] = jnp.where(kind == m, mixed_t, jnp.zeros_like(mixed_t))
 
     scatter_q = Scatter(
-        0, scatter_send, scatter_recv, torus, give_q, total_q, held_q, 1024
+        0, scatter_send, scatter_recv, torus, give_q, total_q, held_q, AWAY_Q
     )
     scatter_o = Scatter(
-        STEPS, scatter_send, scatter_recv, torus, give_o, total_o, held_o, width // 2
+        STEPS, scatter_send, scatter_recv, torus, give_o, total_o, held_o, AWAY_O
     )
     tokens = blocks * window
     d_qkv_all = dqkv_s[...].reshape(tokens, 3 * inner)
@@ -454,6 +553,21 @@
             parts.append(ht_s[kind, at, :])
         return nn_dot(jnp.concatenate(parts, axis=0), d_qkv_all)
 
+    cot_all = cot_ref[...].reshape(tokens, width)
+
+    def o_rows(kind, store):
+        below = jnp.zeros((padded - rows, width), F32)
+        for at in range(0, CHIPS, 4):
+            four = nn_dot(mt_s[kind, at * rows : (at + 4) * rows, :], cot_all)
+            for i in range(4):
+                store(at + i, jnp.concatenate([four[i * rows : (i + 1) * rows], below], axis=0))
+
+    def store_given(chip, value):
+        give_o[chip] = value.astype(BF16)
+
+    o_rows(1 - core, store_given)
+    for j in (3, 2, 1, 0):
+        scatter_o.give(j)
     for j in (3, 2, 1, 0):
         found = q_block(1 - core, j)
         for n in range(4):
@@ -465,13 +579,36 @@
         found = q_block(core, j)
         scatter_q.take(j, lambda n, chip: found[n * share : (n + 1) * share])
 
+    gather_o.finish()
+
+    def keep_own(chip, value):
+        wp[core, chip] = value.astype(BF16)
+
+    o_rows(core, keep_own)
+
+    def take_o(j):
+        scatter_o.take(j, lambda n, chip: wp[core, chip].astype(F32))
+
     take_q(3)
+    take_q(2)
+    take_o(3)
+    take_o(2)
+    scatter_q.take_lent(3)
     scatter_q.send_far()
-    take_q(2)
+    scatter_o.take_lent(3)
+    scatter_o.send_far()
+    take_q(1)
+    scatter_q.take_lent(2)
     scatter_q.send_near(2)
-    take_q(1)
+    scatter_q.take_lent(1)
     scatter_q.send_near(1)
     take_q(0)
+    take_o(1)
+    take_o(0)
+    scatter_o.take_lent(2)
+    scatter_o.send_near(2)
+    scatter_o.take_lent(1)
+    scatter_o.send_near(1)
     dgain_s[...] = jnp.zeros_like(dgain_s)
 
     def finish_blocks(low, high):
@@ -481,7 +618,6 @@
             x_hat = xhat_s[b]
             gain = gain_s[kind]
             y = x_ref[b].astype(F32) + nn_dot(mixed_s[b], wo[kind])
-            y_s[b] = y.astype(BF16)
             d_normed = nt_dot(dqkv_s[b], weights(kind, 0, 3 * inner))
             d_gain = jnp.sum(d_normed * x_hat, axis=0, keepdims=True)
             for m in range(2):
@@ -493,57 +629,30 @@
                 - x_hat * jnp.mean(scaled * x_hat, axis=-1, keepdims=True)
             )
             dx_s[b] = (cot_ref[b].astype(F32) + d_input).astype(BF16)
+            xhat_s[b] = y
 
     finish_blocks(0, blocks)
-    cot_all = cot_ref[...].reshape(tokens, width)
-
-    def o_rows(kind, store):
-        below = jnp.concatenate(
-            [dgain_s[kind], jnp.zeros((padded - rows - 1, width), F32)], axis=0
-        )
-        for at in range(0, CHIPS, 4):
-            four = nn_dot(mt_s[kind, at * rows : (at + 4) * rows, :], cot_all)
-            for i in range(4):
-                store(at + i, jnp.concatenate([four[i * rows : (i + 1) * rows], below], axis=0))
-
-    def store_given(chip, value):
-        give_o[chip] = value.astype(BF16)
-
-    o_rows(1 - core, store_given)
-    for j in (3, 2, 1, 0):
-        scatter_o.give(j)
+    gains = Exchange(0, gain_send, gain_recv, torus, gain_sums, gain_rows)
+    gains.begin(dgain_s)
+    scatter_q.take_lent(0)
     scatter_q.first_far()
-    gather_o.finish()
-
-    def keep_own(chip, value):
-        wp[core, chip] = value.astype(BF16)
-
-    o_rows(core, keep_own)
+    gains.step()
+    scatter_o.take_lent(0)
+    scatter_o.first_far()
+    gains.step()
     scatter_q.first_near()
-
-    def take_o(j):
-        scatter_o.take(j, lambda n, chip: wp[core, chip].astype(F32))
-
-    take_o(3)
-    scatter_o.send_far()
-    scatter_q.swap(lambda value: (value[:share // 2], value[share // 2 :]))
-    take_o(2)
-    take_o(1)
-    scatter_o.send_near(2)
-    scatter_o.send_near(1)
-    take_o(0)
-    scatter_q.cross()
+    gains.step()
     for r in range(blocks):
-        y, dx = y_s[0], dx_s[0]
+        y, dx = xhat_s[0], dx_s[0]
         for b in range(1, blocks):
-            y = jnp.where(rank_ref[b] == r, y_s[b], y)
+            y = jnp.where(rank_ref[b] == r, xhat_s[b], y)
             dx = jnp.where(rank_ref[b] == r, dx_s[b], dx)
-        enc_ref[r] = y
+        enc_ref[r] = y.astype(BF16)
         grad_ref[r] = dx
-    scatter_o.first_far()
-    scatter_q.pair_up(out_q)
     scatter_o.first_near()
-
+    gains.step()
+    scatter_q.swap(lambda value: (value[: share // 2], value[share // 2 :]))
+    gains.step()
     def split_o(value):
         half = rows // 2
         below = jnp.concatenate([value[rows : rows + 1], jnp.zeros((3, width), F32)], axis=0)
@@ -553,11 +662,15 @@
         )
 
     scatter_o.swap(split_o)
+    scatter_q.cross()
+    gains.step()
+    scatter_o.cross()
+    scatter_q.pair_up(out_q)
+    scatter_o.pair_up(out_o)
+    gains.end(out_gain)
     scatter_q.end(out_q)
-    scatter_o.cross()
-    scatter_o.pair_up(out_o)
     scatter_o.end(out_o)
-    for one in (early, gather_o, gather_q, scatter_q, scatter_o):
+    for one in (early, gather_o, gather_q, scatter_q, scatter_o, gains):
         one.finish()
 
 
@@ -580,25 +693,34 @@
         pltpu.VMEM((count, window, width), F32),
         pltpu.VMEM((count, window, LANES), F32),
         pltpu.VMEM((window, 3 * inner), BF16),
-        pltpu.VMEM((window, inner), BF16),
+        pltpu.VMEM((count, window, inner), BF16),
         pltpu.VMEM((count, window, inner), BF16),
         pltpu.VMEM((count, window, 3 * inner), BF16),
         pltpu.VMEM((2, width, tokens), BF16),
         pltpu.VMEM((2, inner, tokens), BF16),
         pltpu.VMEM((count, window, width), BF16),
-        pltpu.VMEM((count, window, width), BF16),
         pltpu.VMEM((2, 1, width), F32),
+        pltpu.VMEM((7, 1, width), F32),
+        pltpu.VMEM((8, 1, width), F32),
         pltpu.VMEM((CHIPS,) + q, BF16),
         pltpu.VMEM((CHIPS,) + o, BF16),
         pltpu.VMEM((CHIPS,) + q, BF16),
         pltpu.VMEM((CHIPS,) + o, BF16),
     ]
     for lead in ((4,), (4, 2), (), (2,)):
-        scratch += [pltpu.VMEM(lead + q, BF16), pltpu.VMEM(lead + o, BF16)]
+        scratch += [
+            pltpu.VMEM(lead + (q[0], q[1] - AWAY_Q), BF16),
+            pltpu.VMEM(lead + (o[0], o[1] - AWAY_O), BF16),
+        ]
+    scratch += [
+        pltpu.VMEM((CHIPS, q[0], AWAY_Q), BF16),
+        pltpu.VMEM((CHIPS, o[0], AWAY_O), BF16),
+    ]
     for lead in ((2,), (), (3,)):
         scratch += [pltpu.VMEM(lead + half_q, BF16), pltpu.VMEM(lead + half_o, BF16)]
-    scratch += [pltpu.SemaphoreType.DMA((2 * 32 + 3,))] * 2
+    scratch += [pltpu.SemaphoreType.DMA((2 * 48 + 3,))] * 2
     scratch += [pltpu.SemaphoreType.DMA((2 * STEPS,))] * 2
+    scratch += [pltpu.SemaphoreType.DMA((8,))] * 2
     vmem = pl.BlockSpec(memory_space=pltpu.VMEM)
     return pl.pallas_call(
         layer_kernel,
@@ -607,9 +729,10 @@
             jax.ShapeDtypeStruct(blocks.shape, BF16),
             jax.ShapeDtypeStruct(half_q, F32),
             jax.ShapeDtypeStruct(half_o, F32),
+            jax.ShapeDtypeStruct((1, width), F32),
         ),
         in_specs=[pl.BlockSpec(memory_space=pltpu.SMEM)] * 2 + [vmem] * 5,
-        out_specs=(vmem,) * 4,
+        out_specs=(vmem,) * 5,
         scratch_shapes=scratch,
         compiler_params=pltpu.CompilerParams(
             collective_id=0, has_side_effects=True, vmem_limit_bytes=VMEM_BYTES
@@ -624,10 +747,10 @@
     gain_row = lax.dynamic_update_slice(
         jnp.zeros((2, width), F32), norm_gain.astype(F32), (0, start)
     )[:, None, :]
-    encoded, block_grad, share_qkv, share_packed = layer(
+    encoded, block_grad, share_qkv, share_packed, gains = layer(
         modality, time_rank, blocks, cotangent, qkv_weight, out_weight, gain_row
     )
-    share_gain = lax.dynamic_slice(share_packed, (rows, start), (1, share))
+    share_gain = lax.dynamic_slice(gains, (0, start), (1, share))
     return (encoded, block_grad, share_qkv[None], share_packed[None, :rows], share_gain)
 
 

time: 142 us -> 147 us (1.035)
  Pallas kernels: 131 us -> 136 us
    pallas_call x1, Pallas kernels: 131 us -> 136 us  [layer(): pl.pallas_call(layer_kernel, out_shape=(jax.ShapeDtypeStruct(blocks.shape...]
where the time goes in v4:
time: 147 us
  Pallas kernels  136 us (93%)
  local copies, waits for them, and re-layouts  9.1 us (6%)
    pallas_call x1, Pallas kernels, layer(): pl.pallas_call(layer_kernel, out_shape=(jax.ShapeDtypeStruct(blocks.shape...  136 us
    unnamed x11, local copies, waits for them, and re-layouts  6.75 us

profile of v4, /device:TPU:2, one launch (start us, length us, event | category | flops | bytes accessed | tf_op | source)
XLA Modules:
  0.0 146.6 jit_solution(12765654626582758655)
XLA Ops:
  0.6 0.7 bitcast_convert_fusion
  1.3 0.2 dynamic_update_slice.4.gain_in
  1.5 0.0 copy-start.2
  1.5 1.6 %copy.13.o_in = bf16[2,20,1280]{2,1,0:T(8,128)(2,1)} copy(bf16[2,20,1280]{2,0,1:T(2,128)(2,1)} %param.12) | data formatting | bytes 204800 | tf_op args[5]
  3.0 0.0 copy-done.2
  3.1 136.2 %shard_map.110 = (bf16[4,128,1280]{2,1,0:T(8,128)(2,1)}, bf16[4,128,1280]{2,1,0:T(8,128)(2,1)}, f32[40,1920]{1,0:T(8,128)}, f32[24,1280]{1,0:T(8,128)}, f32[1,1280]{1,0:T(1,128)}) custom-call(s32[4]{0:T(128)} %kind_ref.1, s32[4]{0:T(128)} %rank_ref.1, bf16[4,128,1280]{2,1,0:T(8,128)(2,1)} %x_ref.1, bf16[4,128,1280]{2,1,0:T(8,128)(2,1)} %cot_ref.1, ...), custom_call_target="tpu_custom_call" | custom-call | tf_op jit(solution)/shard_map/pallas_call | solution.py:725
  139.3 1.3 constant_dynamic-slice_fusion
  140.5 0.9 slice_bitcast_fusion
  141.4 0.7 copy.14
  142.2 0.0 copy-start
  142.2 2.6 %copy.19 = bf16[4,128,1280]{2,1,0:T(8,128)(2,1)} copy(bf16[4,128,1280]{2,1,0:T(8,128)(2,1)} %get-tuple-element.25) | data formatting | bytes 2621440
  144.7 0.0 copy-done
  144.7 0.0 copy-start.1
  144.7 1.1 copy.20
  145.8 0.1 copy-done.1
  145.9 0.7 copy.21
  (1 shorter events, 0.0 us)
Async XLA Ops:
  1.5 1.6 %copy-start.2 = (f32[2,1,1280]{2,1,0:T(1,128)}, f32[2,1,1280]{2,1,0:T(1,128)S(1)}, u32[]{:S(2)}) copy-start(f32[2,1,1280]{2,1,0:T(1,128)S(1)} %dynamic_update_slice.4.gain_in) | copy-start | bytes 30724
  142.2 2.6 %copy-start = (bf16[4,128,1280]{2,1,0:T(8,128)(2,1)S(1)}, bf16[4,128,1280]{2,1,0:T(8,128)(2,1)}, u32[]{:S(2)}) copy-start(bf16[4,128,1280]{2,1,0:T(8,128)(2,1)} %get-tuple-element.26) | copy-start | bytes 3932164
  144.7 1.2 copy-start.1

commit v5 on v3

--- a/solution.py
+++ b/solution.py
@@ -18,7 +18,9 @@
 VMEM_BYTES = 62 * 1024 * 1024
 RING = 4
 CHIPS = RING * RING
-STEPS = 35
+STEPS = 51
+BEHIND = 6
+AWAY_Q, AWAY_O = 5 * LANES, 3 * LANES
 MESH = pl.DeviceIdType.MESH
 OFFSETS = (0, -1, 1, 2)
 UP = (True, False, False, True)
@@ -173,86 +175,125 @@
         self.sent = []
 
 
-class Gather(Lane):
-    def __init__(self, base, send_sem, recv_sem, torus, held, cut):
+class Slots(Lane):
+    def __init__(self, base, send_sem, recv_sem, torus, columns, away):
         super().__init__(base, send_sem, recv_sem, torus.sibling)
-        self.torus, self.held, self.cut = torus, held, cut
-
-    def slot(self, n, j, kind=None):
-        kind = self.torus.core if kind is None else kind
-        return self.held.at[kind, self.torus.chip(OFFSETS[n], OFFSETS[j], kind)]
+        self.torus, self.away, self.carried = torus, away, columns - away
+        odd = torus.row % 2
+        self.start = pl.multiple_of(away * (1 - odd), LANES)
+        self.missing = pl.ds(pl.multiple_of(self.carried * odd, LANES), away)
+        self.lent = pl.ds(pl.multiple_of(self.carried * (1 - odd), LANES), away)
+        self.cut = -(-self.carried // (2 * LANES)) * LANES
+
+    def chip(self, n, j):
+        return self.torus.chip(OFFSETS[n], OFFSETS[j], self.torus.core)
+
+    def window(self):
+        return pl.ds(self.start, self.carried)
+
+    def half_window(self, upper):
+        if upper:
+            return pl.ds(self.start + self.cut, self.carried - self.cut)
+        return pl.ds(self.start, self.cut)
+
+    def neighbour(self, n, j):
+        return self.torus.across if (n + j) % 2 else self.torus.beside
+
+
+class Gather(Slots):
+    def __init__(self, base, send_sem, recv_sem, torus, held, away, pending):
+        super().__init__(base, send_sem, recv_sem, torus, held.shape[-1], away)
+        self.held, self.pending = held, pending
+
+    def slot(self, n, j, columns=None):
+        columns = self.window() if columns is None else columns
+        return self.held.at[self.torus.core, self.chip(n, j), :, columns]
 
     def half(self, n, upper):
-        low = self.cut if upper else 0
-        size = self.held.shape[-1] - self.cut if upper else self.cut
-        chip = self.torus.chip(OFFSETS[n], 0, self.torus.core)
-        return self.held.at[self.torus.core, chip, :, pl.ds(low, size)]
+        return self.slot(n, 0, self.half_window(upper))
 
     def pass_on(self, number, view, first_by, second_by):
         self.send(number, view, view, self.torus.near(first_by, second_by))
 
     def share(self, n, j):
-        view = self.slot(n, j)
+        view = self.held.at[self.torus.core, self.chip(n, j)]
         self.send(16 + 4 * n + j, view, view, self.sibling)
+
+    def lend(self, n, j):
+        view = self.slot(n, j, self.lent)
+        self.send(32 + 4 * n + j, view, view, self.neighbour(n, j))
+        self.pending.append((self, n, j))
+        if len(self.pending) > BEHIND:
+            one, n, j = self.pending.pop(0)
+            one.complete(n, j)
+
+    def complete(self, n, j):
+        self.arrive(32 + 4 * n + j, self.slot(n, j, self.missing))
+        self.share(n, j)
 
     def along_second(self, n):
         self.pass_on(4 + 2 * n, self.slot(n, 0), 0, 1)
         self.pass_on(5 + 2 * n, self.slot(n, 0), 0, -1)
-        self.share(n, 0)
 
     def begin(self):
         self.pass_on(0, self.slot(0, 0), 1, 0)
         self.pass_on(1, self.slot(0, 0), -1, 0)
         self.along_second(0)
+        self.share(0, 0)
 
     def ring_back(self):
         self.arrive(0, self.slot(1, 0))
         self.pass_on(2, self.half(1, False), 1, 0)
         self.along_second(1)
+        self.lend(1, 0)
 
     def ring_ahead(self):
         self.arrive(1, self.slot(2, 0))
         self.pass_on(3, self.half(2, True), -1, 0)
         self.along_second(2)
+        self.lend(2, 0)
 
     def ring_far(self):
         self.arrive(2, self.half(3, False))
         self.arrive(3, self.half(3, True))
         self.along_second(3)
+        self.lend(3, 0)
 
     def second_near(self, n):
         self.arrive(4 + 2 * n, self.slot(n, 1))
         if UP[n]:
             self.pass_on(12 + n, self.slot(n, 1), 0, 1)
-        self.share(n, 1)
+        self.lend(n, 1)
         self.arrive(5 + 2 * n, self.slot(n, 2))
         if not UP[n]:
             self.pass_on(12 + n, self.slot(n, 2), 0, -1)
-        self.share(n, 2)
+        self.lend(n, 2)
 
     def second_far(self, n):
         self.arrive(12 + n, self.slot(n, 3))
-        self.share(n, 3)
+        self.lend(n, 3)
 
     def other_kind(self):
+        other = 1 - self.torus.core
         for j in range(4):
             for n in range(4):
-                self.arrive(16 + 4 * n + j, self.slot(n, j, 1 - self.torus.core))
-
-
-class Scatter(Lane):
-    def __init__(self, base, send_sem, recv_sem, torus, given, total, held, cut):
-        super().__init__(base, send_sem, recv_sem, torus.sibling)
-        self.torus, self.given, self.total, self.cut = torus, given, total, cut
-        self.one, self.two, self.three, self.four, self.kinds, self.leave, self.row_in = held
-
-    def at(self, n, j):
-        return self.torus.chip(OFFSETS[n], OFFSETS[j], self.torus.core)
-
-    def part(self, ref, upper):
-        low = self.cut if upper else 0
-        size = ref.shape[-1] - self.cut if upper else self.cut
-        return ref.at[:, pl.ds(low, size)]
+                chip = self.torus.chip(OFFSETS[n], OFFSETS[j], other)
+                self.arrive(16 + 4 * n + j, self.held.at[other, chip])
+
+
+class Scatter(Slots):
+    def __init__(self, base, send_sem, recv_sem, torus, given, total, held, away):
+        super().__init__(base, send_sem, recv_sem, torus, total.shape[-1], away)
+        self.given, self.total = given, total
+        self.one, self.two, self.three, self.four, self.lent_in = held[:5]
+        self.kinds, self.leave, self.row_in = held[5:]
+
+    def view(self, n, j, columns=None):
+        columns = self.window() if columns is None else columns
+        return self.total.at[self.chip(n, j), :, columns]
+
+    def part(self, upper):
+        return self.three.at[:, slice(self.cut, None) if upper else slice(0, self.cut)]
 
     def add(self, target, *terms):
         value = target[...].astype(F32)
@@ -267,71 +308,78 @@
 
     def take(self, j, own):
         for n in range(4):
-            chip = self.at(n, j)
+            chip = self.chip(n, j)
             self.arrive(4 * j + n, self.total.at[chip])
             value = own(n, chip) + self.total[chip].astype(F32)
             self.total[chip] = value.astype(BF16)
+            if n or j:
+                lent = self.view(n, j, self.missing)
+                self.send(32 + 4 * j + n, lent, self.lent_in.at[4 * j + n], self.neighbour(n, j))
+
+    def take_lent(self, j):
+        for n in range(4):
+            if n or j:
+                self.arrive(32 + 4 * j + n, self.lent_in.at[4 * j + n])
+                self.add(self.view(n, j, self.lent), self.lent_in.at[4 * j + n])
 
     def send_far(self):
         for n in range(4):
             device = self.torus.near(0, 1 if UP[n] else -1)
-            self.send(16 + n, self.total.at[self.at(n, 3)], self.one.at[n], device)
+            self.send(16 + n, self.view(n, 3), self.one.at[n], device)
 
     def send_near(self, j):
         for n in (3, 1, 2, 0):
             if UP[n] == (j == 2):
                 self.arrive(16 + n, self.one.at[n])
-                self.add(self.total.at[self.at(n, j)], self.one.at[n])
+                self.add(self.view(n, j), self.one.at[n])
             number, which = (20 + 2 * n, 0) if j == 2 else (21 + 2 * n, 1)
             device = self.torus.near(0, OFFSETS[j])
-            self.send(number, self.total.at[self.at(n, j)], self.two.at[n, which], device)
+            self.send(number, self.view(n, j), self.two.at[n, which], device)
 
     def close_second(self, n):
         self.arrive(20 + 2 * n, self.two.at[n, 0])
         self.arrive(21 + 2 * n, self.two.at[n, 1])
-        self.add(self.total.at[self.at(n, 0)], self.two.at[n, 0], self.two.at[n, 1])
+        self.add(self.view(n, 0), self.two.at[n, 0], self.two.at[n, 1])
 
     def first_far(self):
         self.close_second(3)
-        view = self.total.at[self.at(3, 0)]
-        self.send(28, self.part(view, False), self.part(self.three, False), self.torus.near(1, 0))
-        self.send(29, self.part(view, True), self.part(self.three, True), self.torus.near(-1, 0))
+        for upper, by in ((False, 1), (True, -1)):
+            view = self.view(3, 0, self.half_window(upper))
+            self.send(28 + upper, view, self.part(upper), self.torus.near(by, 0))
         for n in (2, 1, 0):
             self.close_second(n)
 
     def first_near(self):
         for n, upper, by in ((2, False, 1), (1, True, -1)):
-            view = self.total.at[self.at(n, 0)]
-            self.arrive(28 + upper, self.part(self.three, upper))
-            self.add(self.part(view, upper), self.part(self.three, upper))
-            self.send(30 + upper, view, self.four.at[int(upper)], self.torus.near(by, 0))
+            self.arrive(28 + upper, self.part(upper))
+            self.add(self.view(n, 0, self.half_window(upper)), self.part(upper))
+            self.send(30 + upper, self.view(n, 0), self.four.at[int(upper)], self.torus.near(by, 0))
 
     def swap(self, split):
-        view = self.total.at[self.at(0, 0)]
         self.arrive(30, self.four.at[0])
         self.arrive(31, self.four.at[1])
-        value = view[...].astype(F32) + self.four[0].astype(F32) + self.four[1].astype(F32)
-        low, high = split(value)
+        self.add(self.view(0, 0), self.four.at[0], self.four.at[1])
+        low, high = split(self.total[self.chip(0, 0)].astype(F32))
         core = self.torus.core
         self.kinds[core] = jnp.where(core == 0, low, high).astype(BF16)
         self.leave[...] = jnp.where(core == 0, high, low).astype(BF16)
-        self.send(32, self.leave, self.kinds.at[core], self.sibling)
+        self.send(48, self.leave, self.kinds.at[core], self.sibling)
 
     def cross(self):
         kind = self.torus.row // 2
-        self.arrive(32, self.kinds.at[1 - self.torus.core])
-        self.send(33, self.kinds.at[1 - kind], self.row_in.at[0], self.torus.across)
+        self.arrive(48, self.kinds.at[1 - self.torus.core])
+        self.send(49, self.kinds.at[1 - kind], self.row_in.at[0], self.torus.across)
 
     def pair_up(self, out):
         kind = self.torus.row // 2
-        self.arrive(33, self.row_in.at[0])
+        self.arrive(49, self.row_in.at[0])
         value = self.kinds[kind].astype(F32) + self.row_in[0].astype(F32)
         out[...] = value
         self.row_in[1] = value.astype(BF16)
-        self.send(34, self.row_in.at[1], self.row_in.at[2], self.torus.beside)
+        self.send(50, self.row_in.at[1], self.row_in.at[2], self.torus.beside)
 
     def end(self, out):
-        self.arrive(34, self.row_in.at[2])
+        self.arrive(50, self.row_in.at[2])
         out[...] += self.row_in[2].astype(F32)
 
 
@@ -341,8 +389,8 @@
     wq, wp, wo, gain_s, sib_q, sib_o, sib_gain, xhat_s, inv_s, qkv_s, dattn_s, mixed_s, dqkv_s, ht_s, mt_s,
     y_s, dx_s, dgain_s, give_q, give_o, total_q, total_o, *rest,
 ):
-    held_q, held_o = rest[0:14:2], rest[1:14:2]
-    gather_send, gather_recv, scatter_send, scatter_recv = rest[14:]
+    held_q, held_o = rest[0:16:2], rest[1:16:2]
+    gather_send, gather_recv, scatter_send, scatter_recv = rest[16:]
     blocks, window, width = x_ref.shape
     inner = wo.shape[1]
     rows = inner // CHIPS
@@ -353,12 +401,13 @@
     core = torus.core
     first = core == 0
 
-    early = Lane(2 * 32, gather_send, gather_recv, torus.sibling)
+    early = Lane(2 * 48, gather_send, gather_recv, torus.sibling)
     early.send(0, o_in.at[1 - core], sib_o, torus.sibling)
     early.send(1, gain_in.at[1 - core], sib_gain, torus.sibling)
     early.send(2, q_in.at[1 - core], sib_q, torus.sibling)
-    gather_o = Gather(0, gather_send, gather_recv, torus, wp, width // 2)
-    gather_q = Gather(32, gather_send, gather_recv, torus, wq, 1024)
+    pending = []
+    gather_o = Gather(0, gather_send, gather_recv, torus, wp, AWAY_O, pending)
+    gather_q = Gather(48, gather_send, gather_recv, torus, wq, AWAY_Q, pending)
     gathers = (gather_o, gather_q)
     here = torus.y * RING + torus.z
     early.arrive(0, sib_o)
@@ -407,6 +456,8 @@
         one.second_far(1)
         one.second_far(2)
         one.second_far(3)
+    for one, n, j in pending:
+        one.complete(n, j)
     gather_o.other_kind()
 
     @pl.loop(0, 2)
@@ -438,10 +489,10 @@
             mt_s[m, :, columns] = jnp.where(kind == m, mixed_t, jnp.zeros_like(mixed_t))
 
     scatter_q = Scatter(
-        0, scatter_send, scatter_recv, torus, give_q, total_q, held_q, 1024
+        0, scatter_send, scatter_recv, torus, give_q, total_q, held_q, AWAY_Q
     )
     scatter_o = Scatter(
-        STEPS, scatter_send, scatter_recv, torus, give_o, total_o, held_o, width // 2
+        STEPS, scatter_send, scatter_recv, torus, give_o, total_o, held_o, AWAY_O
     )
     tokens = blocks * window
     d_qkv_all = dqkv_s[...].reshape(tokens, 3 * inner)
@@ -466,10 +517,13 @@
         scatter_q.take(j, lambda n, chip: found[n * share : (n + 1) * share])
 
     take_q(3)
+    take_q(2)
+    scatter_q.take_lent(3)
     scatter_q.send_far()
-    take_q(2)
+    take_q(1)
+    scatter_q.take_lent(2)
     scatter_q.send_near(2)
-    take_q(1)
+    scatter_q.take_lent(1)
     scatter_q.send_near(1)
     take_q(0)
     dgain_s[...] = jnp.zeros_like(dgain_s)
@@ -512,27 +566,30 @@
     o_rows(1 - core, store_given)
     for j in (3, 2, 1, 0):
         scatter_o.give(j)
-    scatter_q.first_far()
     gather_o.finish()
 
     def keep_own(chip, value):
         wp[core, chip] = value.astype(BF16)
 
     o_rows(core, keep_own)
-    scatter_q.first_near()
 
     def take_o(j):
         scatter_o.take(j, lambda n, chip: wp[core, chip].astype(F32))
 
     take_o(3)
+    take_o(2)
+    scatter_o.take_lent(3)
     scatter_o.send_far()
-    scatter_q.swap(lambda value: (value[:share // 2], value[share // 2 :]))
-    take_o(2)
     take_o(1)
+    take_o(0)
+    scatter_q.take_lent(0)
+    scatter_q.first_far()
+    scatter_o.take_lent(2)
     scatter_o.send_near(2)
+    scatter_o.take_lent(1)
     scatter_o.send_near(1)
-    take_o(0)
-    scatter_q.cross()
+    scatter_q.first_near()
+    scatter_o.take_lent(0)
     for r in range(blocks):
         y, dx = y_s[0], dx_s[0]
         for b in range(1, blocks):
@@ -541,8 +598,9 @@
         enc_ref[r] = y
         grad_ref[r] = dx
     scatter_o.first_far()
-    scatter_q.pair_up(out_q)
+    scatter_q.swap(lambda value: (value[: share // 2], value[share // 2 :]))
     scatter_o.first_near()
+    scatter_q.cross()
 
     def split_o(value):
         half = rows // 2
@@ -553,9 +611,10 @@
         )
 
     scatter_o.swap(split_o)
-    scatter_q.end(out_q)
+    scatter_q.pair_up(out_q)
     scatter_o.cross()
     scatter_o.pair_up(out_o)
+    scatter_q.end(out_q)
     scatter_o.end(out_o)
     for one in (early, gather_o, gather_q, scatter_q, scatter_o):
         one.finish()
@@ -594,10 +653,17 @@
         pltpu.VMEM((CHIPS,) + o, BF16),
     ]
     for lead in ((4,), (4, 2), (), (2,)):
-        scratch += [pltpu.VMEM(lead + q, BF16), pltpu.VMEM(lead + o, BF16)]
+        scratch += [
+            pltpu.VMEM(lead + (q[0], q[1] - AWAY_Q), BF16),
+            pltpu.VMEM(lead + (o[0], o[1] - AWAY_O), BF16),
+        ]
+    scratch += [
+        pltpu.VMEM((CHIPS, q[0], AWAY_Q), BF16),
+        pltpu.VMEM((CHIPS, o[0], AWAY_O), BF16),
+    ]
     for lead in ((2,), (), (3,)):
         scratch += [pltpu.VMEM(lead + half_q, BF16), pltpu.VMEM(lead + half_o, BF16)]
-    scratch += [pltpu.SemaphoreType.DMA((2 * 32 + 3,))] * 2
+    scratch += [pltpu.SemaphoreType.DMA((2 * 48 + 3,))] * 2
     scratch += [pltpu.SemaphoreType.DMA((2 * STEPS,))] * 2
     vmem = pl.BlockSpec(memory_space=pltpu.VMEM)
     return pl.pallas_call(

time: 142 us -> 139 us (0.979)
  Pallas kernels: 131 us -> 128 us
    pallas_call x1, Pallas kernels: 131 us -> 128 us  [layer(): pl.pallas_call(layer_kernel, out_shape=(jax.ShapeDtypeStruct(blocks.shape...]
where the time goes in v5:
time: 139 us
  Pallas kernels  128 us (92%)
  local copies, waits for them, and re-layouts  9.12 us (7%)
    pallas_call x1, Pallas kernels, layer(): pl.pallas_call(layer_kernel, out_shape=(jax.ShapeDtypeStruct(blocks.shape...  128 us
    unnamed x11, local copies, waits for them, and re-layouts  6.75 us

profile of v5, /device:TPU:2, one launch (start us, length us, event | category | flops | bytes accessed | tf_op | source)
XLA Modules:
  0.0 138.8 jit_solution(3990504078807703257)
XLA Ops:
  0.6 0.7 bitcast_convert_fusion
  1.3 0.2 dynamic_update_slice.4.gain_in
  1.5 0.0 copy-start.2
  1.5 1.6 %copy.13.o_in = bf16[2,20,1280]{2,1,0:T(8,128)(2,1)} copy(bf16[2,20,1280]{2,0,1:T(2,128)(2,1)} %param.12) | data formatting | bytes 204800 | tf_op args[5]
  3.0 0.0 copy-done.2
  3.1 128.4 %shard_map.110 = (bf16[4,128,1280]{2,1,0:T(8,128)(2,1)}, bf16[4,128,1280]{2,1,0:T(8,128)(2,1)}, f32[40,1920]{1,0:T(8,128)}, f32[24,1280]{1,0:T(8,128)}) custom-call(s32[4]{0:T(128)} %kind_ref.1, s32[4]{0:T(128)} %rank_ref.1, bf16[4,128,1280]{2,1,0:T(8,128)(2,1)} %x_ref.1, bf16[4,128,1280]{2,1,0:T(8,128)(2,1)} %cot_ref.1, bf16[2,40,1920]{2,1,0:T(8,128)(2,1)} %q_in.1, ...), custom_call_target="tpu_custom_call" | custom-call | tf_op jit(solution)/shard_map/pallas_call | solution.py:669
  131.4 1.3 constant_dynamic-slice_fusion
  132.7 0.9 slice_bitcast_fusion
  133.6 0.7 copy.14
  134.4 0.0 copy-start
  134.4 2.6 %copy.19 = bf16[4,128,1280]{2,1,0:T(8,128)(2,1)} copy(bf16[4,128,1280]{2,1,0:T(8,128)(2,1)} %get-tuple-element.23) | data formatting | bytes 2621440
  136.9 0.0 copy-done
  136.9 0.0 copy-start.1
  136.9 1.1 copy.20
  138.0 0.1 copy-done.1
  138.1 0.7 copy.21
  (1 shorter events, 0.0 us)
Async XLA Ops:
  1.5 1.6 %copy-start.2 = (f32[2,1,1280]{2,1,0:T(1,128)}, f32[2,1,1280]{2,1,0:T(1,128)S(1)}, u32[]{:S(2)}) copy-start(f32[2,1,1280]{2,1,0:T(1,128)S(1)} %dynamic_update_slice.4.gain_in) | copy-start | bytes 30724
  134.4 2.6 %copy-start = (bf16[4,128,1280]{2,1,0:T(8,128)(2,1)S(1)}, bf16[4,128,1280]{2,1,0:T(8,128)(2,1)}, u32[]{:S(2)}) copy-start(bf16[4,128,1280]{2,1,0:T(8,128)(2,1)} %get-tuple-element.24) | copy-start | bytes 3932164
  136.9 1.2 copy-start.1

commit v6 on v5

--- a/solution.py
+++ b/solution.py
@@ -387,7 +387,7 @@
     kind_ref, rank_ref, x_ref, cot_ref, q_in, o_in, gain_in,
     enc_ref, grad_ref, out_q, out_o,
     wq, wp, wo, gain_s, sib_q, sib_o, sib_gain, xhat_s, inv_s, qkv_s, dattn_s, mixed_s, dqkv_s, ht_s, mt_s,
-    y_s, dx_s, dgain_s, give_q, give_o, total_q, total_o, *rest,
+    y_s, dx_s, enc_s, grad_s, out_sem, dgain_s, give_q, give_o, total_q, total_o, *rest,
 ):
     held_q, held_o = rest[0:16:2], rest[1:16:2]
     gather_send, gather_recv, scatter_send, scatter_recv = rest[16:]
@@ -590,13 +590,17 @@
     scatter_o.send_near(1)
     scatter_q.first_near()
     scatter_o.take_lent(0)
+    leaving = []
     for r in range(blocks):
         y, dx = y_s[0], dx_s[0]
         for b in range(1, blocks):
             y = jnp.where(rank_ref[b] == r, y_s[b], y)
             dx = jnp.where(rank_ref[b] == r, dx_s[b], dx)
-        enc_ref[r] = y
-        grad_ref[r] = dx
+        enc_s[r] = y
+        grad_s[r] = dx
+        for number, (held, ref) in enumerate(((enc_s, enc_ref), (grad_s, grad_ref))):
+            leaving.append(pltpu.make_async_copy(held.at[r], ref.at[r], out_sem.at[2 * r + number]))
+            leaving[-1].start()
     scatter_o.first_far()
     scatter_q.swap(lambda value: (value[: share // 2], value[share // 2 :]))
     scatter_o.first_near()
@@ -616,6 +620,8 @@
     scatter_o.pair_up(out_o)
     scatter_q.end(out_q)
     scatter_o.end(out_o)
+    for made in leaving:
+        made.wait()
     for one in (early, gather_o, gather_q, scatter_q, scatter_o):
         one.finish()
 
@@ -646,6 +652,9 @@
         pltpu.VMEM((2, inner, tokens), BF16),
         pltpu.VMEM((count, window, width), BF16),
         pltpu.VMEM((count, window, width), BF16),
+        pltpu.VMEM((count, window, width), BF16),
+        pltpu.VMEM((count, window, width), BF16),
+        pltpu.SemaphoreType.DMA((2 * count,)),
         pltpu.VMEM((2, 1, width), F32),
         pltpu.VMEM((CHIPS,) + q, BF16),
         pltpu.VMEM((CHIPS,) + o, BF16),
@@ -675,7 +684,7 @@
             jax.ShapeDtypeStruct(half_o, F32),
         ),
         in_specs=[pl.BlockSpec(memory_space=pltpu.SMEM)] * 2 + [vmem] * 5,
-        out_specs=(vmem,) * 4,
+        out_specs=(pl.BlockSpec(memory_space=pl.ANY),) * 2 + (vmem,) * 2,
         scratch_shapes=scratch,
         compiler_params=pltpu.CompilerParams(
             collective_id=0, has_side_effects=True, vmem_limit_bytes=VMEM_BYTES

time: 139 us -> 138 us (level)
  no operation moved by 1% of the time
where the time goes in v6:
time: 138 us
  Pallas kernels  128 us (93%)
  local copies, waits for them, and re-layouts  9.12 us (7%)
    pallas_call x1, Pallas kernels, layer(): pl.pallas_call(layer_kernel, out_shape=(jax.ShapeDtypeStruct(blocks.shape...  128 us
    unnamed x11, local copies, waits for them, and re-layouts  6.75 us

profile of v6, /device:TPU:2, one launch (start us, length us, event | category | flops | bytes accessed | tf_op | source)
XLA Modules:
  0.0 138.0 jit_solution(11818549380371311368)
XLA Ops:
  0.6 0.7 bitcast_convert_fusion
  1.3 0.2 dynamic_update_slice.4.gain_in
  1.5 0.0 copy-start.2
  1.5 1.6 %copy.13.o_in = bf16[2,20,1280]{2,1,0:T(8,128)(2,1)} copy(bf16[2,20,1280]{2,0,1:T(2,128)(2,1)} %param.12) | data formatting | bytes 204800 | tf_op args[5]
  3.0 0.0 copy-done.2
  3.1 127.6 %shard_map.110 = (bf16[4,128,1280]{2,1,0:T(8,128)(2,1)}, bf16[4,128,1280]{2,1,0:T(8,128)(2,1)}, f32[40,1920]{1,0:T(8,128)}, f32[24,1280]{1,0:T(8,128)}) custom-call(s32[4]{0:T(128)} %kind_ref.1, s32[4]{0:T(128)} %rank_ref.1, bf16[4,128,1280]{2,1,0:T(8,128)(2,1)} %x_ref.1, bf16[4,128,1280]{2,1,0:T(8,128)(2,1)} %cot_ref.1, bf16[2,40,1920]{2,1,0:T(8,128)(2,1)} %q_in.1, ...), custom_call_target="tpu_custom_call" | custom-call | tf_op jit(solution)/shard_map/pallas_call | solution.py:678
  130.7 1.3 constant_dynamic-slice_fusion
  131.9 0.9 slice_bitcast_fusion
  132.9 0.7 copy.14
  133.6 0.0 copy-start
  133.6 2.6 %copy.19 = bf16[4,128,1280]{2,1,0:T(8,128)(2,1)} copy(bf16[4,128,1280]{2,1,0:T(8,128)(2,1)} %get-tuple-element.23) | data formatting | bytes 2621440
  136.2 0.0 copy-done
  136.2 0.0 copy-start.1
  136.2 1.1 copy.20
  137.2 0.1 copy-done.1
  137.3 0.7 copy.21
  (1 shorter events, 0.0 us)
Async XLA Ops:
  1.5 1.6 %copy-start.2 = (f32[2,1,1280]{2,1,0:T(1,128)}, f32[2,1,1280]{2,1,0:T(1,128)S(1)}, u32[]{:S(2)}) copy-start(f32[2,1,1280]{2,1,0:T(1,128)S(1)} %dynamic_update_slice.4.gain_in) | copy-start | bytes 30724
  133.6 2.6 %copy-start = (bf16[4,128,1280]{2,1,0:T(8,128)(2,1)S(1)}, bf16[4,128,1280]{2,1,0:T(8,128)(2,1)}, u32[]{:S(2)}) copy-start(bf16[4,128,1280]{2,1,0:T(8,128)(2,1)} %get-tuple-element.24) | copy-start | bytes 3932164
  136.2 1.2 copy-start.1
